TPU v7x, 128 devices: a whole 4x4x4 slice. The times are simulated.
128 devices in a mesh: chan: 16 (over y_lo, z, core), lag: 8 (over y_hi, x).
Axes of the slice: x: 4, y: 4 (y_hi: 2, y_lo: 2; y = y_hi * 2 + y_lo), z: 4, core: 2. Of those that a mesh axis runs over, the one named last changes fastest.
Arguments:
- raw: bfloat16 [4096, 40000], P('chan', 'lag'), may hold values from -720 to 720
- fir_taps: bfloat16 [80], replicated, may hold values from -0.625 to 0.625
- channel_map: int32 [4096], P('chan'), may hold values from 0 to 4095, as said below
- lag_offsets: int32 [32], P('lag'), may hold values from -40 to 40, as said below
Outputs:
- correlation: float32 [4096, 32, 4096], P('chan', 'lag')
Inputs may be any that keep to these rules, and one draw needn't show every extreme that they name: A permutation of the channels that keeps each channel in its aligned group of 256: channel_map[c] // 256 == c // 256. `lag_offsets`: distinct values; both ends of the range are taken.
All inputs are finite; a program needn't handle non-finite values.
Results may differ from a plain program's by a relative error of at most 0.004.
Values may be sent and summed in bfloat16 or wider, within the bound.
A program may use at most 256 MiB of HBM per device.

v0:
```python
import math

import jax
import jax.numpy as jnp
from jax import lax
from jax.sharding import PartitionSpec as P

DEC = 20
MAXLAG = 40


def shifted_2(value, axis, by):
    peers = lax.axis_size(axis)
    return lax.ppermute(value, axis, [(i, (i + by) % peers) for i in range(peers)])


def decimate(series, lead_cols, fir_taps):
    joined = jnp.concatenate([lead_cols, series], axis=1)
    blocks = joined.reshape(joined.shape[0], -1, DEC)
    tap_table = fir_taps[::-1].reshape(-1, DEC)
    out_len = series.shape[1] // DEC
    summed = jnp.zeros((series.shape[0], out_len), jnp.float32)
    for index in range(tap_table.shape[0]):
        summed = summed + jnp.einsum(
            "cnr,r->cn",
            blocks[:, index : index + out_len, :],
            tap_table[index],
            preferred_element_type=jnp.float32,
        )
    return summed


def whiten(decimated):
    average = jnp.mean(decimated, axis=1, keepdims=True)
    centred = decimated - average
    energy = jnp.mean(centred * centred, axis=1, keepdims=True)
    return (centred * lax.rsqrt(energy + 1e-05)).astype(jnp.bfloat16)


def reorder(block_series, targets):
    source = (
        jnp.zeros(targets.shape, jnp.int32)
        .at[targets]
        .set(jnp.arange(targets.shape[0], dtype=jnp.int32))
    )
    return jnp.take(block_series, source, axis=0)


def correlate(own_rows, remote, lag_offsets):
    width = own_rows.shape[1]
    padded = jnp.pad(remote, ((0, 0), (MAXLAG, MAXLAG)))
    shifted = jnp.stack(
        [
            lax.dynamic_slice_in_dim(padded, lag_offsets[slot] + MAXLAG, width, 1)
            for slot in range(lag_offsets.shape[0])
        ]
    )
    product = jnp.einsum("it,ljt->ilj", own_rows, shifted, preferred_element_type=jnp.float32)
    return product * (1.0 / math.sqrt(width))


def local(raw, fir_taps, channel_map, lag_offsets):
    chan_count = lax.axis_size("chan")
    chan_index = lax.axis_index("chan")
    block_size = channel_map.shape[0]
    lead_width = fir_taps.shape[0] - DEC
    series = lax.all_to_all(raw, "lag", split_axis=0, concat_axis=1, tiled=True)
    lead_cols = jnp.zeros((series.shape[0], lead_width), series.dtype)
    decimated = decimate(series, lead_cols, fir_taps)
    whitened = whiten(decimated)
    result = jnp.zeros((block_size, lag_offsets.shape[0], block_size * chan_count), jnp.float32)

    def place(total, tile_corr, block_index):
        return lax.dynamic_update_slice(total, tile_corr, (0, 0, block_index * block_size))

    own_rows = reorder(
        lax.all_gather(whitened, "lag", axis=0, tiled=True), channel_map - chan_index * block_size
    )
    result = place(result, correlate(own_rows, own_rows, lag_offsets), chan_index)

    def advance(turn, loop_state):
        current, total = loop_state
        current = shifted_2(current, "chan", 1)
        block_index = jnp.mod(chan_index - turn, chan_count)
        return (current, place(total, correlate(own_rows, current, lag_offsets), block_index))

    loop_state = lax.fori_loop(1, chan_count, advance, (own_rows, result))
    result = loop_state[1]
    return result


def solution(mesh):
    placed = (P("chan", "lag"), P(), P("chan"), P("lag"))
    return jax.shard_map(
        local, mesh=mesh, in_specs=placed, out_specs=P("chan", "lag", None), check_vma=False
    )
```

profile of v0, /device:TPU:0, one launch (start us, length us, event | category | flops | bytes accessed | tf_op | source)
XLA Modules:
  0.0 477.7 jit_solution(13374261010015945863)
XLA Ops:
  0.0 4.4 copy.14
  4.4 7.0 %all-to-all-start = ((bf16[8,32,5000]{2,1,0:T(8,128)(2,1)}), bf16[8,32,5000]{2,1,0:T(8,128)(2,1)S(1)}, u32[]{:S(2)}, u32[]{:S(2)}) async-start(bf16[8,32,5000]{2,1,0:T(8,128)(2,1)} %bitcast.68), calls=%async_computation | async-start | bytes 5242880 | tf_op jit(solution)/shard_map/all_to_all | solution.py:67
  19.1 26.4 %all-to-all-done = bf16[8,32,5000]{2,1,0:T(8,128)(2,1)S(1)} async-done(((bf16[8,32,5000]{2,1,0:T(8,128)(2,1)}), bf16[8,32,5000]{2,1,0:T(8,128)(2,1)S(1)}, u32[]{:S(2)}, u32[]{:S(2)}) %all-to-all-start) | async-done | bytes 2560032 | tf_op jit(solution)/shard_map/all_to_all | solution.py:67
  45.5 2.9 copy.15
  48.4 6.5 %all_to_all.17 = bf16[32,40000]{1,0:T(8,128)(2,1)} reshape(bf16[32,8,5000]{2,1,0:T(8,128)(2,1)} %copy.15) | data formatting | bytes 5120000 | tf_op jit(solution)/shard_map/all_to_all | solution.py:67
  55.0 2.5 concatenate.3
  57.4 15.3 %reshape.48 = bf16[32,2003,20]{2,1,0:T(8,128)(2,1)} reshape(bf16[32,40060]{1,0:T(8,128)(2,1)S(1)} %concatenate.3) | data formatting | bytes 5127680 | tf_op jit(solution)/shard_map/reshape | solution.py:19
  72.7 10.6 %fusion.19 = f32[1,32,2000]{2,0,1:T(1,128)S(1)} fusion(bf16[32,2003,20]{2,1,0:T(8,128)(2,1)} %reshape.48, bf16[20]{0:T(256)(128)(2,1)S(1)} %slice.91), kind=kOutput, calls=%fused_computation.19 | convolution fusion | flops 2560000 | bytes 16640040 | tf_op jit(solution)/shard_map/cnr,r->cn/dot_general | solution.py:24
  83.3 5.1 %fusion.21 = f32[1,32,2000]{2,0,1:T(1,128)S(1)} fusion(bf16[32,2003,20]{2,1,0:T(8,128)(2,1)S(1)} %copy-done.1, bf16[20]{0:T(256)(128)(2,1)S(1)} %slice.88), kind=kOutput, calls=%fused_computation.21 | convolution fusion | flops 2560000 | bytes 16640512 | tf_op jit(solution)/shard_map/cnr,r->cn/dot_general | solution.py:24
  88.4 4.9 %fusion.23 = f32[1,32,2000]{2,0,1:T(1,128)S(1)} fusion(bf16[32,2003,20]{2,1,0:T(8,128)(2,1)S(1)} %copy-done.1, bf16[20]{0:T(256)(128)(2,1)S(1)} %slice.85), kind=kOutput, calls=%fused_computation.23 | convolution fusion | flops 2560000 | bytes 16640512 | tf_op jit(solution)/shard_map/cnr,r->cn/dot_general | solution.py:24
  93.4 4.9 %fusion.25 = f32[1,32,2000]{2,0,1:T(1,128)S(1)} fusion(bf16[32,2003,20]{2,1,0:T(8,128)(2,1)S(1)} %copy-done.1, bf16[20]{0:T(256)(128)(2,1)S(1)} %slice.82), kind=kOutput, calls=%fused_computation.25 | convolution fusion | flops 2560000 | bytes 16640512 | tf_op jit(solution)/shard_map/cnr,r->cn/dot_general | solution.py:24
  99.1 38.4 %all_gather.3 = bf16[256,2000]{1,0:T(8,128)(2,1)S(1)} all-gather(bf16[32,2000]{1,0:T(8,128)(2,1)S(1)} %multiply_convert_fusion), channel_id=1, replica_groups=mesh['chan'=16,'lag'=8] {'lag'}, dimensions={0}, use_global_device_ids=true | all-gather | bytes 1152000 | tf_op jit(solution)/shard_map/all_gather | solution.py:77
  141.9 3.7 pad_dynamic-slice_fusion.3
  152.3 2.8 fusion.35
  156.9 5.7 %copy-done = f32[256,4,4096]{0,2,1:T(8,128)} copy-done((f32[256,4,4096]{0,2,1:T(8,128)}, f32[256,4,4096]{0,2,1:T(8,128)S(1)}, u32[]{:S(2)}) %copy-start) | copy-done | bytes 16777240
  162.6 294.9 %while.18 = (s32[]{:T(128)}, bf16[256,2000]{0,1:T(8,128)(2,1)S(1)}, f32[256,4,4096]{0,2,1:T(8,128)}, s32[]{:T(128)}, s32[]{:T(128)}, /*index=5*/s32[]{:T(128)}, ...) while((s32[]{:T(128)}, bf16[256,2000]{0,1:T(8,128)(2,1)S(1)}, ...), condition=%wide.region_4.5_spmd, body=%wide.region_3.4_spmd.sunk | while | flops 1054982144 | bytes 17432944 | solution.py:87
  162.6 16.0 %collective-permute-done = bf16[256,2000]{0,1:T(8,128)(2,1)S(1)} collective-permute-done((bf16[256,2000]{0,1:T(8,128)(2,1)S(1)}, bf16[256,2000]{0,1:T(8,128)(2,1)S(1)}, u32[]{:S(2)}, u32[]{:S(2)}) %collective-permute-start) | collective-permute-done | bytes 1024032 | tf_op jit(solution)/shard_map/while/body/eval_jaxpr/ppermute | solution.py:14
  182.3 16.0 %collective-permute-done = bf16[256,2000]{0,1:T(8,128)(2,1)S(1)} collective-permute-done((bf16[256,2000]{0,1:T(8,128)(2,1)S(1)}, bf16[256,2000]{0,1:T(8,128)(2,1)S(1)}, u32[]{:S(2)}, u32[]{:S(2)}) %collective-permute-start) | collective-permute-done | bytes 1024032 | tf_op jit(solution)/shard_map/while/body/eval_jaxpr/ppermute | solution.py:14
  202.0 16.0 %collective-permute-done = bf16[256,2000]{0,1:T(8,128)(2,1)S(1)} collective-permute-done((bf16[256,2000]{0,1:T(8,128)(2,1)S(1)}, bf16[256,2000]{0,1:T(8,128)(2,1)S(1)}, u32[]{:S(2)}, u32[]{:S(2)}) %collective-permute-start) | collective-permute-done | bytes 1024032 | tf_op jit(solution)/shard_map/while/body/eval_jaxpr/ppermute | solution.py:14
  221.6 16.0 %collective-permute-done = bf16[256,2000]{0,1:T(8,128)(2,1)S(1)} collective-permute-done((bf16[256,2000]{0,1:T(8,128)(2,1)S(1)}, bf16[256,2000]{0,1:T(8,128)(2,1)S(1)}, u32[]{:S(2)}, u32[]{:S(2)}) %collective-permute-start) | collective-permute-done | bytes 1024032 | tf_op jit(solution)/shard_map/while/body/eval_jaxpr/ppermute | solution.py:14
  241.3 16.0 %collective-permute-done = bf16[256,2000]{0,1:T(8,128)(2,1)S(1)} collective-permute-done((bf16[256,2000]{0,1:T(8,128)(2,1)S(1)}, bf16[256,2000]{0,1:T(8,128)(2,1)S(1)}, u32[]{:S(2)}, u32[]{:S(2)}) %collective-permute-start) | collective-permute-done | bytes 1024032 | tf_op jit(solution)/shard_map/while/body/eval_jaxpr/ppermute | solution.py:14
  261.0 16.0 %collective-permute-done = bf16[256,2000]{0,1:T(8,128)(2,1)S(1)} collective-permute-done((bf16[256,2000]{0,1:T(8,128)(2,1)S(1)}, bf16[256,2000]{0,1:T(8,128)(2,1)S(1)}, u32[]{:S(2)}, u32[]{:S(2)}) %collective-permute-start) | collective-permute-done | bytes 1024032 | tf_op jit(solution)/shard_map/while/body/eval_jaxpr/ppermute | solution.py:14
  280.6 16.0 %collective-permute-done = bf16[256,2000]{0,1:T(8,128)(2,1)S(1)} collective-permute-done((bf16[256,2000]{0,1:T(8,128)(2,1)S(1)}, bf16[256,2000]{0,1:T(8,128)(2,1)S(1)}, u32[]{:S(2)}, u32[]{:S(2)}) %collective-permute-start) | collective-permute-done | bytes 1024032 | tf_op jit(solution)/shard_map/while/body/eval_jaxpr/ppermute | solution.py:14
  300.3 16.0 %collective-permute-done = bf16[256,2000]{0,1:T(8,128)(2,1)S(1)} collective-permute-done((bf16[256,2000]{0,1:T(8,128)(2,1)S(1)}, bf16[256,2000]{0,1:T(8,128)(2,1)S(1)}, u32[]{:S(2)}, u32[]{:S(2)}) %collective-permute-start) | collective-permute-done | bytes 1024032 | tf_op jit(solution)/shard_map/while/body/eval_jaxpr/ppermute | solution.py:14
  319.9 16.0 %collective-permute-done = bf16[256,2000]{0,1:T(8,128)(2,1)S(1)} collective-permute-done((bf16[256,2000]{0,1:T(8,128)(2,1)S(1)}, bf16[256,2000]{0,1:T(8,128)(2,1)S(1)}, u32[]{:S(2)}, u32[]{:S(2)}) %collective-permute-start) | collective-permute-done | bytes 1024032 | tf_op jit(solution)/shard_map/while/body/eval_jaxpr/ppermute | solution.py:14
  339.6 16.0 %collective-permute-done = bf16[256,2000]{0,1:T(8,128)(2,1)S(1)} collective-permute-done((bf16[256,2000]{0,1:T(8,128)(2,1)S(1)}, bf16[256,2000]{0,1:T(8,128)(2,1)S(1)}, u32[]{:S(2)}, u32[]{:S(2)}) %collective-permute-start) | collective-permute-done | bytes 1024032 | tf_op jit(solution)/shard_map/while/body/eval_jaxpr/ppermute | solution.py:14
  359.3 16.0 %collective-permute-done = bf16[256,2000]{0,1:T(8,128)(2,1)S(1)} collective-permute-done((bf16[256,2000]{0,1:T(8,128)(2,1)S(1)}, bf16[256,2000]{0,1:T(8,128)(2,1)S(1)}, u32[]{:S(2)}, u32[]{:S(2)}) %collective-permute-start) | collective-permute-done | bytes 1024032 | tf_op jit(solution)/shard_map/while/body/eval_jaxpr/ppermute | solution.py:14
  379.0 16.0 %collective-permute-done = bf16[256,2000]{0,1:T(8,128)(2,1)S(1)} collective-permute-done((bf16[256,2000]{0,1:T(8,128)(2,1)S(1)}, bf16[256,2000]{0,1:T(8,128)(2,1)S(1)}, u32[]{:S(2)}, u32[]{:S(2)}) %collective-permute-start) | collective-permute-done | bytes 1024032 | tf_op jit(solution)/shard_map/while/body/eval_jaxpr/ppermute | solution.py:14
  398.7 16.0 %collective-permute-done = bf16[256,2000]{0,1:T(8,128)(2,1)S(1)} collective-permute-done((bf16[256,2000]{0,1:T(8,128)(2,1)S(1)}, bf16[256,2000]{0,1:T(8,128)(2,1)S(1)}, u32[]{:S(2)}, u32[]{:S(2)}) %collective-permute-start) | collective-permute-done | bytes 1024032 | tf_op jit(solution)/shard_map/while/body/eval_jaxpr/ppermute | solution.py:14
  418.3 16.0 %collective-permute-done = bf16[256,2000]{0,1:T(8,128)(2,1)S(1)} collective-permute-done((bf16[256,2000]{0,1:T(8,128)(2,1)S(1)}, bf16[256,2000]{0,1:T(8,128)(2,1)S(1)}, u32[]{:S(2)}, u32[]{:S(2)}) %collective-permute-start) | collective-permute-done | bytes 1024032 | tf_op jit(solution)/shard_map/while/body/eval_jaxpr/ppermute | solution.py:14
  438.0 16.0 %collective-permute-done = bf16[256,2000]{0,1:T(8,128)(2,1)S(1)} collective-permute-done((bf16[256,2000]{0,1:T(8,128)(2,1)S(1)}, bf16[256,2000]{0,1:T(8,128)(2,1)S(1)}, u32[]{:S(2)}, u32[]{:S(2)}) %collective-permute-start) | collective-permute-done | bytes 1024032 | tf_op jit(solution)/shard_map/while/body/eval_jaxpr/ppermute | solution.py:14
  457.5 20.2 %copy.24 = f32[256,4,4096]{2,1,0:T(4,128)} copy(f32[256,4,4096]{0,2,1:T(8,128)} %get-tuple-element.249) | data formatting | bytes 33554432 | tf_op jit(solution)/shard_map/while | solution.py:87
  (103 shorter events, 69.8 us)
Async XLA Ops:
  0.0 11.4 %copy-start.5 = (s32[4]{0:T(128)S(1)}, s32[4]{0:T(128)}, u32[]{:S(2)}) copy-start(s32[4]{0:T(128)} %param.9) | copy-start | bytes 52
  0.0 17.1 %copy-start.6 = (bf16[80]{0:T(256)(128)(2,1)S(1)}, bf16[80]{0:T(256)(128)(2,1)}, u32[]{:S(2)}) copy-start(bf16[80]{0:T(256)(128)(2,1)} %param.7) | copy-start | bytes 484
  0.0 17.6 %copy-start.7 = (s32[256]{0:T(256)S(1)}, s32[256]{0:T(256)}, u32[]{:S(2)}) copy-start(s32[256]{0:T(256)} %param.8) | copy-start | bytes 3076
  4.4 41.1 %all-to-all-start = ((bf16[8,32,5000]{2,1,0:T(8,128)(2,1)}), bf16[8,32,5000]{2,1,0:T(8,128)(2,1)S(1)}, u32[]{:S(2)}, u32[]{:S(2)}) async-start(bf16[8,32,5000]{2,1,0:T(8,128)(2,1)} %bitcast.68), calls=%async_computation | async-start | bytes 5242880 | tf_op jit(solution)/shard_map/all_to_all | solution.py:67
  72.7 10.6 %copy-start.1 = (bf16[32,2003,20]{2,1,0:T(8,128)(2,1)S(1)}, bf16[32,2003,20]{2,1,0:T(8,128)(2,1)}, u32[]{:S(2)}) copy-start(bf16[32,2003,20]{2,1,0:T(8,128)(2,1)} %reshape.48) | copy-start | bytes 7691524
  139.9 1.0 copy-start.2
  155.4 7.1 %copy-start.3 = (bf16[256,2000]{0,1:T(8,128)(2,1)S(1)}, bf16[256,2000]{0,1:T(8,128)(2,1)}, u32[]{:S(2)}) copy-start(bf16[256,2000]{0,1:T(8,128)(2,1)} %copy-done.2) | copy-start | bytes 3072004
  155.5 7.1 %copy-start.4 = (bf16[256,2000]{0,1:T(8,128)(2,1)S(1)}, bf16[256,2000]{0,1:T(8,128)(2,1)}, u32[]{:S(2)}) copy-start(bf16[256,2000]{0,1:T(8,128)(2,1)} %copy.42) | copy-start | bytes 3072004
  156.9 5.7 %copy-start = (f32[256,4,4096]{0,2,1:T(8,128)}, f32[256,4,4096]{0,2,1:T(8,128)S(1)}, u32[]{:S(2)}) copy-start(f32[256,4,4096]{0,2,1:T(8,128)S(1)} %constant_dynamic-update-slice_fusion) | copy-start | bytes 50331652
  162.6 16.1 %collective-permute-start = (bf16[256,2000]{0,1:T(8,128)(2,1)S(1)}, bf16[256,2000]{0,1:T(8,128)(2,1)S(1)}, u32[]{:S(2)}, u32[]{:S(2)}) collective-permute-start(bf16[256,2000]{0,1:T(8,128)(2,1)S(1)} %get-tuple-element.383), channel_id=1, source_target_pairs={{0,8},{8,16},{16,24},{24,32},{32,40},{40,48},{48,56},{56,64},{64,7... | collective-permute-start | bytes 3072008 | tf_op jit(solution)/shard_map/while/body/eval_jaxpr/ppermute | solution.py:14
  182.2 16.1 %collective-permute-start = (bf16[256,2000]{0,1:T(8,128)(2,1)S(1)}, bf16[256,2000]{0,1:T(8,128)(2,1)S(1)}, u32[]{:S(2)}, u32[]{:S(2)}) collective-permute-start(bf16[256,2000]{0,1:T(8,128)(2,1)S(1)} %get-tuple-element.383), channel_id=1, source_target_pairs={{0,8},{8,16},{16,24},{24,32},{32,40},{40,48},{48,56},{56,64},{64,7... | collective-permute-start | bytes 3072008 | tf_op jit(solution)/shard_map/while/body/eval_jaxpr/ppermute | solution.py:14
  201.9 16.1 %collective-permute-start = (bf16[256,2000]{0,1:T(8,128)(2,1)S(1)}, bf16[256,2000]{0,1:T(8,128)(2,1)S(1)}, u32[]{:S(2)}, u32[]{:S(2)}) collective-permute-start(bf16[256,2000]{0,1:T(8,128)(2,1)S(1)} %get-tuple-element.383), channel_id=1, source_target_pairs={{0,8},{8,16},{16,24},{24,32},{32,40},{40,48},{48,56},{56,64},{64,7... | collective-permute-start | bytes 3072008 | tf_op jit(solution)/shard_map/while/body/eval_jaxpr/ppermute | solution.py:14
  221.5 16.1 %collective-permute-start = (bf16[256,2000]{0,1:T(8,128)(2,1)S(1)}, bf16[256,2000]{0,1:T(8,128)(2,1)S(1)}, u32[]{:S(2)}, u32[]{:S(2)}) collective-permute-start(bf16[256,2000]{0,1:T(8,128)(2,1)S(1)} %get-tuple-element.383), channel_id=1, source_target_pairs={{0,8},{8,16},{16,24},{24,32},{32,40},{40,48},{48,56},{56,64},{64,7... | collective-permute-start | bytes 3072008 | tf_op jit(solution)/shard_map/while/body/eval_jaxpr/ppermute | solution.py:14
  241.2 16.1 %collective-permute-start = (bf16[256,2000]{0,1:T(8,128)(2,1)S(1)}, bf16[256,2000]{0,1:T(8,128)(2,1)S(1)}, u32[]{:S(2)}, u32[]{:S(2)}) collective-permute-start(bf16[256,2000]{0,1:T(8,128)(2,1)S(1)} %get-tuple-element.383), channel_id=1, source_target_pairs={{0,8},{8,16},{16,24},{24,32},{32,40},{40,48},{48,56},{56,64},{64,7... | collective-permute-start | bytes 3072008 | tf_op jit(solution)/shard_map/while/body/eval_jaxpr/ppermute | solution.py:14
  260.8 16.1 %collective-permute-start = (bf16[256,2000]{0,1:T(8,128)(2,1)S(1)}, bf16[256,2000]{0,1:T(8,128)(2,1)S(1)}, u32[]{:S(2)}, u32[]{:S(2)}) collective-permute-start(bf16[256,2000]{0,1:T(8,128)(2,1)S(1)} %get-tuple-element.383), channel_id=1, source_target_pairs={{0,8},{8,16},{16,24},{24,32},{32,40},{40,48},{48,56},{56,64},{64,7... | collective-permute-start | bytes 3072008 | tf_op jit(solution)/shard_map/while/body/eval_jaxpr/ppermute | solution.py:14
  280.5 16.1 %collective-permute-start = (bf16[256,2000]{0,1:T(8,128)(2,1)S(1)}, bf16[256,2000]{0,1:T(8,128)(2,1)S(1)}, u32[]{:S(2)}, u32[]{:S(2)}) collective-permute-start(bf16[256,2000]{0,1:T(8,128)(2,1)S(1)} %get-tuple-element.383), channel_id=1, source_target_pairs={{0,8},{8,16},{16,24},{24,32},{32,40},{40,48},{48,56},{56,64},{64,7... | collective-permute-start | bytes 3072008 | tf_op jit(solution)/shard_map/while/body/eval_jaxpr/ppermute | solution.py:14
  300.2 16.1 %collective-permute-start = (bf16[256,2000]{0,1:T(8,128)(2,1)S(1)}, bf16[256,2000]{0,1:T(8,128)(2,1)S(1)}, u32[]{:S(2)}, u32[]{:S(2)}) collective-permute-start(bf16[256,2000]{0,1:T(8,128)(2,1)S(1)} %get-tuple-element.383), channel_id=1, source_target_pairs={{0,8},{8,16},{16,24},{24,32},{32,40},{40,48},{48,56},{56,64},{64,7... | collective-permute-start | bytes 3072008 | tf_op jit(solution)/shard_map/while/body/eval_jaxpr/ppermute | solution.py:14
  319.8 16.1 %collective-permute-start = (bf16[256,2000]{0,1:T(8,128)(2,1)S(1)}, bf16[256,2000]{0,1:T(8,128)(2,1)S(1)}, u32[]{:S(2)}, u32[]{:S(2)}) collective-permute-start(bf16[256,2000]{0,1:T(8,128)(2,1)S(1)} %get-tuple-element.383), channel_id=1, source_target_pairs={{0,8},{8,16},{16,24},{24,32},{32,40},{40,48},{48,56},{56,64},{64,7... | collective-permute-start | bytes 3072008 | tf_op jit(solution)/shard_map/while/body/eval_jaxpr/ppermute | solution.py:14
  339.5 16.1 %collective-permute-start = (bf16[256,2000]{0,1:T(8,128)(2,1)S(1)}, bf16[256,2000]{0,1:T(8,128)(2,1)S(1)}, u32[]{:S(2)}, u32[]{:S(2)}) collective-permute-start(bf16[256,2000]{0,1:T(8,128)(2,1)S(1)} %get-tuple-element.383), channel_id=1, source_target_pairs={{0,8},{8,16},{16,24},{24,32},{32,40},{40,48},{48,56},{56,64},{64,7... | collective-permute-start | bytes 3072008 | tf_op jit(solution)/shard_map/while/body/eval_jaxpr/ppermute | solution.py:14
  359.2 16.1 %collective-permute-start = (bf16[256,2000]{0,1:T(8,128)(2,1)S(1)}, bf16[256,2000]{0,1:T(8,128)(2,1)S(1)}, u32[]{:S(2)}, u32[]{:S(2)}) collective-permute-start(bf16[256,2000]{0,1:T(8,128)(2,1)S(1)} %get-tuple-element.383), channel_id=1, source_target_pairs={{0,8},{8,16},{16,24},{24,32},{32,40},{40,48},{48,56},{56,64},{64,7... | collective-permute-start | bytes 3072008 | tf_op jit(solution)/shard_map/while/body/eval_jaxpr/ppermute | solution.py:14
  378.9 16.1 %collective-permute-start = (bf16[256,2000]{0,1:T(8,128)(2,1)S(1)}, bf16[256,2000]{0,1:T(8,128)(2,1)S(1)}, u32[]{:S(2)}, u32[]{:S(2)}) collective-permute-start(bf16[256,2000]{0,1:T(8,128)(2,1)S(1)} %get-tuple-element.383), channel_id=1, source_target_pairs={{0,8},{8,16},{16,24},{24,32},{32,40},{40,48},{48,56},{56,64},{64,7... | collective-permute-start | bytes 3072008 | tf_op jit(solution)/shard_map/while/body/eval_jaxpr/ppermute | solution.py:14
  398.6 16.1 %collective-permute-start = (bf16[256,2000]{0,1:T(8,128)(2,1)S(1)}, bf16[256,2000]{0,1:T(8,128)(2,1)S(1)}, u32[]{:S(2)}, u32[]{:S(2)}) collective-permute-start(bf16[256,2000]{0,1:T(8,128)(2,1)S(1)} %get-tuple-element.383), channel_id=1, source_target_pairs={{0,8},{8,16},{16,24},{24,32},{32,40},{40,48},{48,56},{56,64},{64,7... | collective-permute-start | bytes 3072008 | tf_op jit(solution)/shard_map/while/body/eval_jaxpr/ppermute | solution.py:14
  418.2 16.1 %collective-permute-start = (bf16[256,2000]{0,1:T(8,128)(2,1)S(1)}, bf16[256,2000]{0,1:T(8,128)(2,1)S(1)}, u32[]{:S(2)}, u32[]{:S(2)}) collective-permute-start(bf16[256,2000]{0,1:T(8,128)(2,1)S(1)} %get-tuple-element.383), channel_id=1, source_target_pairs={{0,8},{8,16},{16,24},{24,32},{32,40},{40,48},{48,56},{56,64},{64,7... | collective-permute-start | bytes 3072008 | tf_op jit(solution)/shard_map/while/body/eval_jaxpr/ppermute | solution.py:14
  437.9 16.1 %collective-permute-start = (bf16[256,2000]{0,1:T(8,128)(2,1)S(1)}, bf16[256,2000]{0,1:T(8,128)(2,1)S(1)}, u32[]{:S(2)}, u32[]{:S(2)}) collective-permute-start(bf16[256,2000]{0,1:T(8,128)(2,1)S(1)} %get-tuple-element.383), channel_id=1, source_target_pairs={{0,8},{8,16},{16,24},{24,32},{32,40},{40,48},{48,56},{56,64},{64,7... | collective-permute-start | bytes 3072008 | tf_op jit(solution)/shard_map/while/body/eval_jaxpr/ppermute | solution.py:14
where the time goes:
time: 478 us
  waiting for transfers between devices  267 us (56%)
  local copies, waits for them, and re-layouts  93.6 us (20%)
  matrix products  63.8 us (13%)
  blocking collectives  38.4 us (8%)
  starting transfers between devices  8.06 us (2%)
  between operations  5.23 us (1%)
    ppermute x15, waiting for transfers between devices, shifted_2(): lax.ppermute(value, axis, [(i, (i + by) % peers) for i in range(peers)])  240 us
    all_gather x1, blocking collectives, local(): lax.all_gather(whitened, 'lag', axis=0, tiled=True)  38.4 us
    dot_general x16, matrix products, correlate(): jnp.einsum('it,ljt->ilj', own_rows, shifted, preferred_element_type=jnp.f...  38.2 us
    all_to_all x1, waiting for transfers between devices, local(): series = lax.all_to_all(raw, 'lag', split_axis=0, concat_axis=1, tiled=True)  26.4 us
    dot_general x4, matrix products, decimate(): jnp.einsum('cnr,r->cn', blocks[:, index:index + out_len, :], tap_table[in...  25.5 us
    while x2, local copies, waits for them, and re-layouts, local(): loop_state = lax.fori_loop(1, chan_count, advance, (own_rows, result))  21.1 us
    another operation x15, local copies, waits for them, and re-layouts, correlate(): jnp.stack([lax.dynamic_slice_in_dim(padded, lag_offsets[slot] + MAXLAG, w...  16.3 us
    reshape x1, local copies, waits for them, and re-layouts, decimate(): blocks = joined.reshape(joined.shape[0], -1, DEC)  15.3 us
  transfers between devices with their start and end apart: 16, of which 16 were waited for; matrix products, arithmetic and copies ran while one was open for 1% of the time, Pallas kernels for 0%

commit v1 on v0

v1 whole, which is shorter than its diff:
```python
import functools
import math

import jax
import jax.numpy as jnp
from jax import lax
from jax.experimental import pallas as pl
from jax.experimental.pallas import tpu as pltpu
from jax.sharding import PartitionSpec as P

MESH = pl.DeviceIdType.MESH
DEC = 20
TAPS = 80
MAXLAG = 40
CB = 256
SAMPLES = 2000
CHANNELS = 4096
SLOTS = 4
STEP = 250
HEAD = 3
ROWS = 5000
F32, BF16 = jnp.float32, jnp.bfloat16

EARLY = 12
COPIES = (
    ((0, 0, 1), 2, 0, 256), ((0, 0, 2), 2, 0, 256), ((0, 0, 3), 2, 0, 256), ((0, 1, 0), 1, 0, 256),
    ((0, 1, 1), 1, 0, 80), ((0, 1, 1), 2, 80, 176), ((0, 1, 2), 1, 0, 80), ((0, 1, 2), 2, 80, 176),
    ((0, 1, 3), 1, 0, 80), ((0, 1, 3), 2, 80, 176), ((0, 2, 0), 1, 0, 256), ((0, 2, 1), 1, 0, 80),
    ((0, 2, 1), 2, 80, 176), ((0, 2, 2), 1, 0, 80), ((0, 2, 2), 2, 80, 176), ((0, 2, 3), 1, 0, 80),
    ((0, 2, 3), 2, 80, 176), ((0, 3, 0), 1, 0, 256), ((0, 3, 1), 1, 0, 80), ((0, 3, 1), 2, 80, 176),
    ((0, 3, 2), 1, 0, 80), ((0, 3, 2), 2, 80, 176), ((0, 3, 3), 1, 0, 80), ((0, 3, 3), 2, 80, 176),
    ((1, 0, 0), 0, 0, 256), ((1, 0, 1), 0, 0, 80), ((1, 0, 1), 0, 160, 96), ((1, 0, 1), 2, 80, 80),
    ((1, 0, 2), 0, 0, 80), ((1, 0, 2), 0, 160, 96), ((1, 0, 2), 2, 80, 80), ((1, 0, 3), 0, 0, 80),
    ((1, 0, 3), 0, 160, 96), ((1, 0, 3), 2, 80, 80), ((1, 1, 0), 1, 0, 160), ((1, 1, 0), 0, 160, 96),
    ((1, 1, 1), 1, 0, 80), ((1, 1, 1), 1, 160, 96), ((1, 1, 1), 2, 80, 80), ((1, 1, 2), 1, 0, 80),
    ((1, 1, 2), 2, 80, 80), ((1, 1, 2), 0, 160, 96), ((1, 1, 3), 1, 0, 80), ((1, 1, 3), 2, 80, 80),
    ((1, 1, 3), 0, 160, 96), ((1, 2, 0), 1, 0, 160), ((1, 2, 0), 0, 160, 96), ((1, 2, 1), 1, 0, 80),
    ((1, 2, 1), 2, 80, 176), ((1, 2, 2), 1, 0, 80), ((1, 2, 2), 2, 80, 80), ((1, 2, 2), 0, 160, 96),
    ((1, 2, 3), 1, 0, 80), ((1, 2, 3), 2, 80, 176), ((1, 3, 0), 1, 0, 160), ((1, 3, 0), 0, 160, 96),
    ((1, 3, 1), 1, 0, 80), ((1, 3, 1), 1, 160, 96), ((1, 3, 1), 2, 80, 80), ((1, 3, 2), 1, 0, 80),
    ((1, 3, 2), 2, 80, 80), ((1, 3, 2), 0, 160, 96), ((1, 3, 3), 1, 0, 80), ((1, 3, 3), 2, 80, 80),
    ((1, 3, 3), 0, 160, 96), ((2, 0, 0), 0, 0, 256), ((2, 0, 1), 0, 0, 80), ((2, 0, 1), 0, 160, 96),
    ((2, 0, 1), 2, 80, 80), ((2, 0, 2), 0, 0, 80), ((2, 0, 2), 0, 160, 96), ((2, 0, 2), 2, 80, 80),
    ((2, 0, 3), 0, 0, 80), ((2, 0, 3), 0, 160, 96), ((2, 0, 3), 2, 80, 80), ((2, 1, 0), 1, 0, 160),
    ((2, 1, 0), 0, 160, 96), ((2, 1, 1), 1, 0, 80), ((2, 1, 1), 2, 80, 80), ((2, 1, 1), 0, 160, 96),
    ((2, 1, 2), 1, 0, 80), ((2, 1, 2), 2, 80, 80), ((2, 1, 2), 0, 160, 96), ((2, 1, 3), 1, 0, 80),
    ((2, 1, 3), 2, 80, 80), ((2, 1, 3), 0, 160, 96), ((2, 2, 0), 1, 0, 160), ((2, 2, 0), 0, 160, 96),
    ((2, 2, 1), 1, 0, 80), ((2, 2, 1), 2, 80, 80), ((2, 2, 1), 0, 160, 96), ((2, 2, 2), 1, 0, 80),
    ((2, 2, 2), 2, 80, 80), ((2, 2, 2), 0, 160, 96), ((2, 2, 3), 1, 0, 80), ((2, 2, 3), 2, 80, 80),
    ((2, 2, 3), 0, 160, 96), ((2, 3, 0), 1, 0, 160), ((2, 3, 0), 0, 160, 96), ((2, 3, 1), 1, 0, 80),
    ((2, 3, 1), 2, 80, 80), ((2, 3, 1), 0, 160, 96), ((2, 3, 2), 1, 0, 80), ((2, 3, 2), 2, 80, 80),
    ((2, 3, 2), 0, 160, 96), ((2, 3, 3), 1, 0, 80), ((2, 3, 3), 2, 80, 80), ((2, 3, 3), 0, 160, 96),
    ((3, 0, 0), 0, 0, 256), ((3, 0, 1), 0, 0, 80), ((3, 0, 1), 0, 160, 96), ((3, 0, 1), 2, 80, 80),
    ((3, 0, 2), 0, 0, 80), ((3, 0, 2), 0, 160, 96), ((3, 0, 2), 2, 80, 80), ((3, 0, 3), 0, 0, 80),
    ((3, 0, 3), 0, 160, 96), ((3, 0, 3), 2, 80, 80), ((3, 1, 0), 1, 0, 160), ((3, 1, 0), 0, 160, 96),
    ((3, 1, 1), 1, 0, 80), ((3, 1, 1), 2, 80, 80), ((3, 1, 1), 0, 160, 96), ((3, 1, 2), 1, 0, 80),
    ((3, 1, 2), 2, 80, 80), ((3, 1, 2), 0, 160, 96), ((3, 1, 3), 1, 0, 80), ((3, 1, 3), 2, 80, 80),
    ((3, 1, 3), 0, 160, 96), ((3, 2, 0), 1, 0, 160), ((3, 2, 0), 0, 160, 96), ((3, 2, 1), 1, 0, 80),
    ((3, 2, 1), 2, 80, 80), ((3, 2, 1), 0, 160, 96), ((3, 2, 2), 1, 0, 80), ((3, 2, 2), 2, 80, 80),
    ((3, 2, 2), 0, 160, 96), ((3, 2, 3), 1, 0, 80), ((3, 2, 3), 2, 80, 80), ((3, 2, 3), 0, 160, 96),
    ((3, 3, 0), 1, 0, 160), ((3, 3, 0), 0, 160, 96), ((3, 3, 1), 1, 0, 80), ((3, 3, 1), 2, 80, 80),
    ((3, 3, 1), 0, 160, 96), ((3, 3, 2), 1, 0, 80), ((3, 3, 2), 2, 80, 80), ((3, 3, 2), 0, 160, 96),
    ((3, 3, 3), 1, 0, 80), ((3, 3, 3), 2, 80, 80), ((3, 3, 3), 0, 160, 96),
)
ACTIONS = (
    ("s", 108), ("s", 17), ("s", 0), ("s", 24), ("s", 3), ("s", 2), ("y", (0, 0, 0)), ("w", 108), ("s", 65),
    ("w", 17), ("s", 10), ("s", 19), ("w", 0), ("s", 109), ("s", 140), ("s", 23), ("s", 25), ("y", (0, 0, 1)),
    ("y", (0, 3, 0)), ("y", (3, 0, 0)), ("s", 111), ("s", 141), ("s", 18), ("s", 117), ("s", 118), ("s", 110),
    ("w", 24), ("s", 27), ("w", 3), ("y", (0, 1, 0)), ("y", (1, 0, 0)), ("w", 2), ("y", (0, 0, 3)), ("s", 1),
    ("s", 115), ("s", 54), ("s", 119), ("s", 31), ("w", 65), ("y", (2, 0, 0)), ("s", 97), ("w", 10),
    ("y", (0, 2, 0)), ("s", 12), ("s", 130), ("w", 109), ("s", 66), ("w", 140), ("s", 129), ("s", 5), ("s", 46),
    ("w", 18), ("w", 19), ("y", (0, 3, 1)), ("w", 141), ("y", (3, 3, 0)), ("s", 35), ("w", 25), ("s", 56),
    ("w", 110), ("w", 111), ("y", (3, 0, 1)), ("s", 16), ("s", 142), ("s", 55), ("s", 34), ("w", 115), ("s", 72),
    ("w", 118), ("w", 119), ("y", (3, 1, 0)), ("s", 9), ("s", 76), ("w", 1), ("y", (0, 0, 2)), ("w", 54), ("s", 45),
    ("s", 112), ("s", 68), ("w", 130), ("s", 87), ("w", 97), ("s", 86), ("s", 58), ("w", 12), ("s", 133),
    ("w", 129), ("y", (3, 2, 0)), ("s", 132), ("s", 98), ("w", 66), ("s", 99), ("s", 100), ("s", 75), ("s", 26),
    ("w", 55), ("y", (1, 3, 0)), ("s", 121), ("w", 16), ("s", 14), ("w", 5), ("s", 122), ("w", 34), ("w", 35),
    ("y", (1, 1, 0)), ("s", 11), ("s", 144), ("w", 56), ("s", 47), ("s", 38), ("s", 67), ("w", 45), ("w", 46),
    ("y", (1, 2, 0)), ("w", 142), ("s", 131), ("s", 48), ("s", 116), ("s", 22), ("w", 86), ("w", 87),
    ("y", (2, 2, 0)), ("w", 133), ("s", 90), ("w", 31), ("s", 62), ("L", 0), ("s", 139), ("w", 99), ("s", 88),
    ("s", 89), ("s", 28), ("w", 72), ("s", 105), ("w", 75), ("s", 78), ("w", 112), ("s", 69), ("s", 148),
    ("s", 143), ("w", 122), ("s", 79), ("s", 4), ("w", 9), ("s", 7), ("w", 144), ("s", 101), ("s", 36), ("w", 23),
    ("s", 21), ("s", 128), ("w", 26), ("s", 37), ("s", 57), ("w", 11), ("y", (0, 2, 1)), ("w", 22),
    ("y", (0, 3, 3)), ("w", 27), ("y", (1, 0, 1)), ("w", 48), ("w", 47), ("y", (1, 2, 1)), ("w", 67), ("w", 68),
    ("y", (2, 0, 1)), ("w", 76), ("y", (2, 1, 0)), ("w", 98), ("y", (2, 3, 0)), ("w", 116), ("w", 117),
    ("y", (3, 0, 3)), ("w", 131), ("w", 132), ("y", (3, 2, 1)), ("s", 150), ("s", 77), ("s", 33), ("s", 32),
    ("w", 88), ("w", 89), ("w", 90), ("y", (2, 2, 1)), ("s", 120), ("s", 53), ("C", 0), ("s", 73), ("s", 15),
    ("s", 74), ("w", 139), ("s", 96), ("w", 62), ("s", 52), ("s", 95), ("s", 113), ("w", 105), ("s", 94), ("w", 4),
    ("y", (0, 1, 1)), ("w", 143), ("y", (3, 3, 1)), ("w", 148), ("s", 137), ("w", 100), ("w", 101),
    ("y", (2, 3, 1)), ("w", 14), ("s", 136), ("s", 138), ("D", 0), ("s", 44), ("s", 20), ("s", 43), ("s", 64),
    ("w", 28), ("s", 59), ("s", 63), ("w", 128), ("s", 85), ("w", 69), ("s", 102), ("s", 84), ("s", 145),
    ("s", 106), ("w", 32), ("w", 33), ("y", (1, 0, 3)), ("w", 36), ("w", 37), ("w", 38), ("y", (1, 1, 1)),
    ("w", 57), ("w", 58), ("y", (1, 3, 1)), ("w", 77), ("w", 78), ("w", 79), ("y", (2, 1, 1)), ("w", 120),
    ("w", 121), ("y", (3, 1, 1)), ("w", 150), ("s", 107), ("s", 8), ("s", 127), ("w", 15), ("y", (0, 2, 3)),
    ("w", 52), ("w", 53), ("y", (1, 2, 3)), ("s", 42), ("w", 7), ("s", 125), ("s", 149), ("w", 73), ("w", 74),
    ("y", (2, 0, 3)), ("C", 1), ("w", 21), ("s", 147), ("s", 83), ("s", 30), ("s", 29), ("s", 126), ("s", 50),
    ("s", 51), ("w", 20), ("s", 13), ("s", 71), ("w", 59), ("s", 49), ("w", 95), ("s", 92), ("y", (0, 3, 2)),
    ("w", 96), ("w", 94), ("y", (2, 2, 3)), ("w", 137), ("w", 138), ("y", (3, 2, 3)), ("w", 113), ("s", 70),
    ("w", 102), ("s", 91), ("s", 114), ("w", 64), ("w", 63), ("y", (1, 3, 3)), ("D", 1), ("w", 136), ("s", 93),
    ("w", 145), ("s", 134), ("s", 135), ("s", 41), ("s", 6), ("w", 43), ("s", 40), ("s", 61), ("s", 39), ("s", 60),
    ("s", 80), ("w", 84), ("s", 81), ("w", 8), ("y", (0, 1, 3)), ("w", 42), ("w", 44), ("y", (1, 1, 3)), ("w", 83),
    ("w", 85), ("y", (2, 1, 3)), ("w", 106), ("w", 107), ("y", (2, 3, 3)), ("w", 126), ("w", 127), ("y", (3, 1, 3)),
    ("w", 149), ("y", (3, 3, 3)), ("w", 125), ("s", 82), ("s", 123), ("s", 103), ("w", 29), ("w", 30),
    ("y", (1, 0, 2)), ("w", 147), ("s", 104), ("w", 13), ("y", (0, 2, 2)), ("s", 124), ("C", 2), ("s", 146),
    ("w", 49), ("w", 50), ("w", 51), ("y", (1, 2, 2)), ("w", 70), ("w", 71), ("y", (2, 0, 2)), ("w", 91), ("w", 92),
    ("w", 93), ("y", (2, 2, 2)), ("w", 114), ("y", (3, 0, 2)), ("w", 134), ("w", 135), ("y", (3, 2, 2)), ("w", 6),
    ("y", (0, 1, 2)), ("D", 2), ("w", 40), ("w", 41), ("w", 39), ("y", (1, 1, 2)), ("w", 60), ("w", 61),
    ("y", (1, 3, 2)), ("w", 80), ("w", 81), ("w", 82), ("y", (2, 1, 2)), ("C", 3), ("w", 104), ("w", 103),
    ("y", (2, 3, 2)), ("w", 123), ("w", 124), ("y", (3, 1, 2)), ("w", 146), ("y", (3, 3, 2)), ("D", 3), ("C", 4),
    ("D", 4), ("C", 5), ("D", 5),
)


def dims():
    chan, lag = lax.axis_index("chan"), lax.axis_index("lag")
    core, z, y_lo = chan % 2, (chan // 2) % 4, chan // 8
    x, y = lag % 4, (lag // 4) * 2 + y_lo
    return x, y, z, core


def device(x, y, z, core):
    return (((y % 2) * 4 + z) * 2 + core, (y // 2) * 4 + x)


def group_channels(coords, group, other):
    _, y, z, core = coords
    ahead = 1 - 2 * core
    sign = -ahead if other else ahead
    z_there = (z + 4 + sign * (0, 1, -1, 2)[group // 2]) % 4
    core_there = 1 - core if other else core
    return (((y + group) % 2) * 4 + z_there) * 2 + core_there


def multiply(lhs_ref, g_ref, channels):
    block = g_ref[pl.ds(channels * 8, 8)].reshape(8 * CB, CB)
    product = jnp.dot(lhs_ref[...], block, preferred_element_type=F32)
    return (product * (1.0 / math.sqrt(SAMPLES))).reshape(CB, SLOTS, CB)


def gather_kernel(
    raw_hbm, taps_ref, map_ref, lags_ref, part_ref, lhs_ref, g_ref,
    raw_ref, dec_ref, stat_ref, turned_ref, shift_ref, mixed_ref,
    raw_sem, stat_send, stat_recv, send_sem, recv_sem, other_send, other_recv,
):
    coords = x, y, z, core = dims()
    me, lag = device(*coords)
    ahead = 1 - 2 * core

    raw_copy = pltpu.make_async_copy(raw_hbm, raw_ref, raw_sem)
    raw_copy.start()

    def lag_peer(step):
        return me, (lag + step) % 8

    sibling = device(x, y, z, 1 - core)
    barrier = pltpu.get_barrier_semaphore()
    peers = [lag_peer(step) for step in range(1, 8)] + [sibling]
    peers += [device(x, (y + step) % 4, z, core) for step in (1, 3)]
    peers += [device(x, y, (z + step) % 4, core) for step in (1, 3)]
    for peer in peers:
        pl.semaphore_signal(barrier, inc=1, device_id=peer, device_id_type=MESH)

    taps = jnp.broadcast_to(taps_ref[...].astype(F32), (8, TAPS)).astype(BF16)
    spread = lax.broadcasted_iota(jnp.int32, (TAPS, 256), 0) + lax.broadcasted_iota(jnp.int32, (TAPS, 256), 1)
    spread = (spread == 128 + DEC - 1).astype(F32).astype(BF16)
    first = jnp.dot(taps, spread, preferred_element_type=F32)
    first = jnp.concatenate([first, jnp.zeros((8, 512), F32)], axis=1)
    wide = lax.broadcasted_iota(jnp.int32, (8, 768), 0)
    band = first
    for step in range(1, 8):
        band = jnp.where(wide == step, pltpu.roll(first, DEC * step, 1), band)
    band = jnp.concatenate([band] + [pltpu.roll(band, 8 * DEC * step, 1) for step in range(1, 4)], axis=0)
    next_band = pltpu.roll(band[0:16, 0:256], 8, 1).astype(BF16)
    band = band.astype(BF16)

    row = lax.broadcasted_iota(jnp.int32, (512, 256), 0)
    far = 10000
    time = jnp.where(
        row < 256,
        jnp.where(row < STEP, row, far),
        jnp.where(row < 384, jnp.where(row - 128 < STEP, row - 128 - STEP, far), row - 384 + STEP),
    )
    column = lax.broadcasted_iota(jnp.int32, (512, 256), 1)
    column = jnp.where(column < STEP, column, -far)
    time = time - column
    for slot in range(SLOTS):
        shift_ref[slot] = (time == -lags_ref[slot]).astype(F32).astype(BF16)

    raw_copy.wait()
    tail = jnp.concatenate([raw_ref[4992:5000].astype(F32), jnp.zeros((8, CB), F32)], axis=0).astype(BF16)
    blank = jnp.zeros((112, CB), BF16)
    window = jnp.concatenate([raw_ref[4864:4992], tail, blank], axis=0)
    over = jnp.dot(next_band, window, preferred_element_type=F32)[0:8]
    for part in range(8):
        begin = 640 * part - 128
        if part == 0:
            piece = jnp.dot(band[:, 128:], raw_ref[0:640], preferred_element_type=F32)
        elif part == 7:
            window = jnp.concatenate([raw_ref[begin:4992], tail, blank], axis=0)
            piece = jnp.dot(band, window, preferred_element_type=F32)
        else:
            piece = jnp.dot(band, raw_ref[begin : begin + 768], preferred_element_type=F32)
        dec_ref[32 * part : 32 * part + 32] = piece

    dec = dec_ref[...]
    sample = lax.broadcasted_iota(jnp.int32, (CB, CB), 0)
    whole = (sample >= HEAD) & (sample < STEP)
    count = STEP - HEAD
    mean = jnp.sum(jnp.where(whole, dec, 0.0), axis=0, keepdims=True) * (1.0 / count)
    spread2 = jnp.where(whole, dec - mean, 0.0)
    energy = jnp.sum(spread2 * spread2, axis=0, keepdims=True)
    line = lax.broadcasted_iota(jnp.int32, (8, CB), 0)
    stat_ref[lag] = jnp.where(
        line == 0,
        mean,
        jnp.where(
            line == 1,
            energy,
            jnp.where(line < 5, pltpu.roll(dec[0:8], 2, 0), pltpu.roll(over, 5, 0)),
        ),
    )
    pl.semaphore_wait(barrier, len(peers))

    def stat_copy(step):
        return pltpu.make_async_remote_copy(
            src_ref=stat_ref.at[lag],
            dst_ref=stat_ref.at[lag],
            send_sem=stat_send.at[step],
            recv_sem=stat_recv.at[step],
            device_id=lag_peer(step),
            device_id_type=MESH,
        )

    for step in range(1, 8):
        stat_copy(step).start()
    order = lax.broadcasted_iota(jnp.int32, (CB, CB), 0)
    place = (map_ref[...] - (me * CB) == order).astype(F32).astype(BF16)
    for step in range(1, 8):
        stat_copy(step).wait_recv()

    stats = [stat_ref[d] for d in range(8)]
    total = jnp.zeros((8, CB), F32)
    heads = []
    before = jnp.zeros((8, CB), F32)
    for d in range(8):
        head = pltpu.roll(stats[d], 6, 0)
        if d:
            from_left = pltpu.roll(stats[d - 1], 3, 0)
            head = head + from_left
            before = before + jnp.where(lag == d, from_left, 0.0)
        heads.append(head)
        total = total + jnp.where(line < HEAD, head, 0.0)
    mean = count * sum(s[0:1] for s in stats) + jnp.sum(total, axis=0, keepdims=True)
    mean = mean * (1.0 / SAMPLES)
    energy = jnp.zeros((1, CB), F32)
    total = jnp.zeros((8, CB), F32)
    for d in range(8):
        away = stats[d][0:1] - mean
        energy = energy + stats[d][1:2] + count * (away * away)
        away = jnp.where(line < HEAD, heads[d] - mean, 0.0)
        total = total + away * away
    energy = (energy + jnp.sum(total, axis=0, keepdims=True)) * (1.0 / SAMPLES)
    scale = lax.rsqrt(energy + 1e-05)
    dec_ref[0:8] = dec_ref[0:8] + jnp.where(line < HEAD, before, 0.0)
    white = jnp.where(sample < STEP, (dec_ref[...] - mean) * scale, 0.0).astype(BF16)
    ordered = lax.dot_general(white, place, (((1,), (1,)), ((), ())), preferred_element_type=F32)

    there = (0, 1, 2, -1)
    at_x = [(x + 4 + ahead * k) % 4 for k in there]
    at_y = [(y + 4 + ahead * k) % 4 for k in there]
    at_z = [(z + 4 + ahead * k) % 4 for k in there]
    term_y = [(k % 2) * 64 + (k // 2) * 4 for k in at_y]
    term_z = [k * 16 + core * 8 for k in at_z]

    def place_of(offset):
        return at_x[offset[0]] + term_y[offset[1]] + term_z[offset[2]]

    neighbours = {}
    for step in (1, 3):
        neighbours[0, step] = device(at_x[step], y, z, core)
        neighbours[1, step] = device(x, at_y[step], z, core)
        neighbours[2, step] = device(x, y, at_z[step], core)

    g_ref[place_of((0, 0, 0))] = ordered.astype(BF16)

    def block_copy(index):
        offset, axis, row, rows = COPIES[index]
        sent = list(offset)
        sent[axis] = {1: 0, 3: 0, 2: 3}[offset[axis]]
        to = 3 if offset[axis] == 1 else 1
        here = g_ref.at[place_of(sent), pl.ds(row, rows)]
        return pltpu.make_async_remote_copy(
            src_ref=here, dst_ref=here, send_sem=send_sem, recv_sem=recv_sem.at[index],
            device_id=neighbours[axis, to], device_id_type=MESH,
        )

    def block_wait(index):
        offset, axis, row, rows = COPIES[index]
        here = g_ref.at[place_of(offset), pl.ds(row, rows)]
        pltpu.make_async_copy(here, here, recv_sem.at[index]).wait()

    def hand_over(offset):
        here = g_ref.at[place_of(offset)]
        group = (at_y[offset[1]] % 2) * 4 + at_z[offset[2]]
        pltpu.make_async_remote_copy(
            src_ref=here, dst_ref=here, send_sem=other_send, recv_sem=other_recv.at[group],
            device_id=sibling, device_id_type=MESH,
        ).start()

    def taken_over(group):
        channels = group_channels(coords, group, True)
        here = g_ref.at[pl.ds(channels * 8, 8)]
        pltpu.make_async_copy(here, here, other_recv.at[channels // 2]).wait()

    def build_own():
        eye = lax.broadcasted_iota(jnp.int32, (CB, CB), 0) == lax.broadcasted_iota(jnp.int32, (CB, CB), 1)
        eye = eye.astype(F32).astype(BF16)
        turned_ref[0] = jnp.zeros((CB, CB), BF16)
        turned_ref[9] = jnp.zeros((CB, CB), BF16)

        def turn(d, carry):
            turned = lax.dot_general(eye, g_ref[me * 8 + d], (((1,), (1,)), ((), ())), preferred_element_type=F32)
            turned_ref[d + 1] = turned.astype(BF16)
            return carry

        lax.fori_loop(0, 8, turn, 0)

        def shift(d, carry):
            around = jnp.concatenate(
                [turned_ref[d + 1], turned_ref[d, :, 128:256], turned_ref[d + 2, :, 0:128]], axis=1
            )
            for slot in range(SLOTS):
                moved = jnp.dot(around, shift_ref[slot], preferred_element_type=F32)
                for half in range(2):
                    mixed_ref[half, pl.ds(slot, CB, stride=SLOTS), :] = moved[:, 128 * half : 128 * half + 128]
            for half in range(2):
                there = pl.ds(pl.multiple_of(d * CB + 128 * half, 128), 128)
                lhs_ref[:, there] = mixed_ref[half].astype(BF16)
            return carry

        lax.fori_loop(0, 8, shift, 0)

    for kind, what in ACTIONS:
        if kind == "w":
            block_wait(what)
        elif kind == "s":
            block_copy(what).start()
        elif kind == "y":
            hand_over(what)
        elif kind == "L":
            build_own()
        elif kind == "C":
            part_ref[2 * what] = multiply(lhs_ref, g_ref, group_channels(coords, what, False))
        elif kind == "D":
            taken_over(what)
            part_ref[2 * what + 1] = multiply(lhs_ref, g_ref, group_channels(coords, what, True))
    for group in range(EARLY // 2, 8):
        taken_over(group)

    for step in range(1, 8):
        stat_copy(step).wait_send()
    gone = g_ref.at[pl.ds(0, 63)]
    pltpu.make_async_copy(gone, gone, send_sem).wait()
    gone = g_ref.at[pl.ds(0, 64)]
    pltpu.make_async_copy(gone, gone, other_send).wait()


def finish_kernel(part_ref, lhs_ref, g_ref, out_ref, stage_ref, part_sem, stage_sem):
    coords = dims()
    late = 16 - EARLY

    def columns(group, other):
        channels = group_channels(coords, group, other)
        return out_ref.at[:, :, pl.ds(pl.multiple_of(channels * CB, CB), CB)]

    def early_copy(index):
        return pltpu.make_async_copy(part_ref.at[index], columns(index // 2, index % 2), part_sem.at[index])

    def late_copy(index):
        there = columns((EARLY + index) // 2, index % 2)
        return pltpu.make_async_copy(stage_ref.at[index], there, stage_sem.at[index])

    for index in range(EARLY):
        early_copy(index).start()
    for index in range(late):
        channels = group_channels(coords, (EARLY + index) // 2, index % 2)
        stage_ref[index] = multiply(lhs_ref, g_ref, channels)
        late_copy(index).start()
    for index in range(EARLY):
        early_copy(index).wait()
    for index in range(late):
        late_copy(index).wait()


def local(raw, fir_taps, channel_map, lag_offsets):
    vmem = pl.BlockSpec(memory_space=pltpu.VMEM)
    part, lhs, blocks = pl.pallas_call(
        gather_kernel,
        out_shape=[
            pltpu.VMEM((EARLY, CB, SLOTS, CB), F32),
            pltpu.VMEM((CB * SLOTS, 8 * CB), BF16),
            pltpu.VMEM((128, CB, CB), BF16),
        ],
        in_specs=[pl.BlockSpec(memory_space=pltpu.HBM), vmem, vmem, pl.BlockSpec(memory_space=pltpu.SMEM)],
        out_specs=[vmem] * 3,
        scratch_shapes=[
            pltpu.VMEM((ROWS, CB), BF16),
            pltpu.VMEM((CB, CB), F32),
            pltpu.VMEM((8, 8, CB), F32),
            pltpu.VMEM((10, CB, CB), BF16),
            pltpu.VMEM((SLOTS, 512, CB), BF16),
            pltpu.VMEM((2, CB * SLOTS, 128), F32),
            pltpu.SemaphoreType.DMA,
            pltpu.SemaphoreType.DMA((8,)),
            pltpu.SemaphoreType.DMA((8,)),
            pltpu.SemaphoreType.DMA,
            pltpu.SemaphoreType.DMA((len(COPIES),)),
            pltpu.SemaphoreType.DMA,
            pltpu.SemaphoreType.DMA((8,)),
        ],
        compiler_params=pltpu.CompilerParams(collective_id=0, has_side_effects=True, vmem_limit_bytes=14 << 20),
        name="gather",
    )(raw.T, fir_taps.reshape(1, TAPS), channel_map.reshape(1, CB), lag_offsets)
    part, lhs, blocks = [pltpu.with_memory_space_constraint(a, pltpu.VMEM) for a in (part, lhs, blocks)]
    return pl.pallas_call(
        finish_kernel,
        out_shape=jax.ShapeDtypeStruct((CB, SLOTS, CHANNELS), F32),
        in_specs=[vmem] * 3,
        out_specs=pl.BlockSpec(memory_space=pltpu.HBM),
        scratch_shapes=[
            pltpu.VMEM((16 - EARLY, CB, SLOTS, CB), F32),
            pltpu.SemaphoreType.DMA((EARLY,)),
            pltpu.SemaphoreType.DMA((16 - EARLY,)),
        ],
        compiler_params=pltpu.CompilerParams(vmem_limit_bytes=(17 - EARLY + 2) << 20),
        name="finish",
    )(part, lhs, blocks)


def solution(mesh):
    placed = (P("chan", "lag"), P(), P("chan"), P("lag"))
    return jax.shard_map(
        local, mesh=mesh, in_specs=placed, out_specs=P("chan", "lag", None), check_vma=False
    )
```

time: 478 us -> 82.9 us (0.17)
  waiting for transfers between devices: 267 us -> 0 us
  local copies, waits for them, and re-layouts: 93.6 us -> 3.71 us
  Pallas kernels: 0 us -> 78.6 us
  matrix products: 63.8 us -> 0 us
  blocking collectives: 38.4 us -> 0 us
  starting transfers between devices: 8.06 us -> 0 us
  between operations: 5.23 us -> 0.19 us
    ppermute x15 -> x0, waiting for transfers between devices: 240 us -> none  [shifted_2(): lax.ppermute(value, axis, [(i, (i + by) % peers) for i in range(peers)])]
    pallas_call x0 -> x2, Pallas kernels: none -> 78.6 us  [the longest x1 70.8 us: local(): pl.pallas_call(gather_kernel, out_shape=[pltpu.VMEM((EARLY, CB, SLOTS, CB...]
    dot_general x20 -> x0, matrix products: 63.8 us -> none  [the longest x16 38.2 us: correlate(): jnp.einsum('it,ljt->ilj', own_rows, shifted, preferred_element_type=jnp.f...]
    all_gather x1 -> x0, blocking collectives: 38.4 us -> none  [local(): lax.all_gather(whitened, 'lag', axis=0, tiled=True)]
    all_to_all x1 -> x0, waiting for transfers between devices: 26.4 us -> none  [local(): series = lax.all_to_all(raw, 'lag', split_axis=0, concat_axis=1, tiled=True)]
    while x17 -> x0, local copies, waits for them, and re-layouts: 22.1 us -> none  [the longest x2 21.1 us: local(): loop_state = lax.fori_loop(1, chan_count, advance, (own_rows, result))]
    another operation x15 -> x0, local copies, waits for them, and re-layouts: 16.3 us -> none  [correlate(): jnp.stack([lax.dynamic_slice_in_dim(padded, lag_offsets[slot] + MAXLAG, w...]
    reshape x1 -> x0, local copies, waits for them, and re-layouts: 15.3 us -> none  [decimate(): blocks = joined.reshape(joined.shape[0], -1, DEC)]
  transfers between devices with their start and end apart: 16 -> 0, of which waited for: 16 -> 0; matrix products, arithmetic and copies ran while one was open for 1% -> 0% of each run, Pallas kernels for 0% -> 0%
where the time goes in v1:
time: 82.9 us; the launch traced here: 82.5 us
  Pallas kernels  78.6 us (95%)
  local copies, waits for them, and re-layouts  3.71 us (4%)
    pallas_call x1, Pallas kernels, local(): pl.pallas_call(gather_kernel, out_shape=[pltpu.VMEM((EARLY, CB, SLOTS, CB...  70.8 us
    pallas_call x1, Pallas kernels, local(): pl.pallas_call(finish_kernel, out_shape=jax.ShapeDtypeStruct((CB, SLOTS,...  7.82 us
    unnamed x8, local copies, waits for them, and re-layouts  3.71 us

profile of v1, /device:TPU:0, one launch (start us, length us, event | category | flops | bytes accessed | tf_op | source)
XLA Modules:
  0.0 82.5 jit_solution(4898112203008362652)
XLA Ops:
  0.0 0.0 copy-start
  0.0 1.7 %copy-done = bf16[256,5000]{0,1:T(8,128)(2,1)S(1)} copy-done((bf16[256,5000]{0,1:T(8,128)(2,1)S(1)}, bf16[256,5000]{0,1:T(8,128)(2,1)}, u32[]{:S(2)}) %copy-start) | copy-done | bytes 2560024
  1.7 0.0 copy-start.1
  1.7 0.7 copy-done.1
  2.4 0.0 copy-start.2
  2.4 0.7 copy-done.2
  3.1 0.0 copy-start.3
  3.1 0.7 copy-done.3
  3.7 70.8 %gather.1 = (f32[12,256,4,256]{3,2,1,0:T(4,128)S(1)}, bf16[1024,2048]{1,0:T(8,128)(2,1)S(1)}, bf16[128,256,256]{2,1,0:T(8,128)(2,1)S(1)}) custom-call(bf16[5000,256]{1,0:T(8,128)(2,1)S(1)} %bitcast.3, bf16[1,80]{1,0:T(2,128)(2,1)S(1)} %bitcast.5, s32[1,256]{1,0:T(1,128)S(1)} %bitcast.4, s32[4]{0:T(128)S(1)} %copy-done.3), custom_call_target="tpu_custom_call" | custom-call | tf_op jit(solution)/shard_map/gather/pallas_call | solution.py:397
  74.5 7.8 %finish.1 = f32[256,4,4096]{2,1,0:T(4,128)} custom-call(f32[12,256,4,256]{3,2,1,0:T(4,128)S(1)} %get-tuple-element.8.part_ref, bf16[1024,2048]{1,0:T(8,128)(2,1)S(1)} %get-tuple-element.9.lhs_ref, bf16[128,256,256]{2,1,0:T(8,128)(2,1)S(1)} %get-tuple-element.10.g_ref), custom_call_target="tpu_custom_call" | custom-call | tf_op jit(solution)/shard_map/finish/pallas_call | solution.py:425
Async XLA Ops:
  0.0 1.7 %copy-start = (bf16[256,5000]{0,1:T(8,128)(2,1)S(1)}, bf16[256,5000]{0,1:T(8,128)(2,1)}, u32[]{:S(2)}) copy-start(bf16[256,5000]{0,1:T(8,128)(2,1)} %param.4) | copy-start | bytes 7680004
  1.7 0.7 copy-start.1
  2.4 0.7 copy-start.2
  3.1 0.7 copy-start.3

commit v2 on v1

v2 whole, which is shorter than its diff:
```python
import functools
import math

import jax
import jax.numpy as jnp
from jax import lax
from jax.experimental import pallas as pl
from jax.experimental.pallas import tpu as pltpu
from jax.sharding import PartitionSpec as P

MESH = pl.DeviceIdType.MESH
DEC = 20
TAPS = 80
MAXLAG = 40
CB = 256
SAMPLES = 2000
CHANNELS = 4096
SLOTS = 4
STEP = 250
HEAD = 3
ROWS = 5000
F32, BF16 = jnp.float32, jnp.bfloat16

EARLY = 12
COPIES = (
    ((0, 0, 1), 2, 0, 256), ((0, 0, 2), 2, 0, 256), ((0, 0, 3), 2, 0, 256), ((0, 1, 0), 1, 0, 256),
    ((0, 1, 1), 2, 0, 256), ((0, 1, 2), 2, 0, 256), ((0, 1, 3), 2, 0, 256), ((0, 2, 0), 1, 0, 256),
    ((0, 2, 1), 1, 0, 256), ((0, 2, 2), 2, 0, 256), ((0, 2, 3), 1, 0, 256), ((0, 3, 0), 1, 0, 256),
    ((0, 3, 1), 2, 0, 256), ((0, 3, 2), 1, 0, 256), ((0, 3, 3), 2, 0, 80), ((0, 3, 3), 2, 160, 96),
    ((0, 3, 3), 1, 80, 80), ((1, 0, 0), 0, 0, 256), ((1, 0, 1), 0, 0, 160), ((1, 0, 1), 2, 160, 96),
    ((1, 0, 2), 2, 0, 256), ((1, 0, 3), 2, 0, 256), ((1, 1, 0), 1, 0, 80), ((1, 1, 0), 0, 80, 176),
    ((1, 1, 1), 1, 0, 256), ((1, 1, 2), 2, 0, 256), ((1, 1, 3), 0, 0, 256), ((1, 2, 0), 1, 0, 160),
    ((1, 2, 0), 0, 160, 96), ((1, 2, 1), 1, 0, 256), ((1, 2, 2), 0, 0, 256), ((1, 2, 3), 1, 0, 256),
    ((1, 3, 0), 1, 0, 160), ((1, 3, 0), 0, 160, 96), ((1, 3, 1), 2, 0, 256), ((1, 3, 2), 2, 0, 256),
    ((1, 3, 3), 0, 0, 256), ((2, 0, 0), 0, 0, 256), ((2, 0, 1), 2, 0, 256), ((2, 0, 2), 2, 0, 256),
    ((2, 0, 3), 0, 0, 256), ((2, 1, 0), 1, 0, 256), ((2, 1, 1), 0, 0, 256), ((2, 1, 2), 1, 0, 256),
    ((2, 1, 3), 0, 0, 256), ((2, 2, 0), 1, 0, 160), ((2, 2, 0), 0, 160, 96), ((2, 2, 1), 2, 0, 256),
    ((2, 2, 2), 1, 0, 256), ((2, 2, 3), 0, 0, 256), ((2, 3, 0), 1, 0, 256), ((2, 3, 1), 2, 0, 256),
    ((2, 3, 2), 1, 0, 256), ((2, 3, 3), 1, 0, 256), ((3, 0, 0), 0, 0, 256), ((3, 0, 1), 0, 0, 256),
    ((3, 0, 2), 0, 0, 256), ((3, 0, 3), 2, 0, 160), ((3, 0, 3), 0, 160, 96), ((3, 1, 0), 0, 0, 256),
    ((3, 1, 1), 2, 0, 256), ((3, 1, 2), 2, 0, 256), ((3, 1, 3), 1, 0, 256), ((3, 2, 0), 1, 0, 160),
    ((3, 2, 0), 0, 160, 96), ((3, 2, 1), 0, 0, 256), ((3, 2, 2), 1, 0, 256), ((3, 2, 3), 0, 0, 256),
    ((3, 3, 0), 0, 0, 256), ((3, 3, 1), 0, 0, 256), ((3, 3, 2), 0, 0, 256), ((3, 3, 3), 1, 0, 256),
)
ACTIONS = (
    ("s", 54), ("s", 11), ("s", 2), ("y", (0, 0, 0)), ("s", 17), ("s", 3), ("s", 0), ("w", 54), ("s", 37),
    ("w", 11), ("s", 7), ("s", 12), ("w", 2), ("y", (0, 0, 3)), ("y", (0, 3, 0)), ("y", (3, 0, 0)), ("s", 68),
    ("s", 16), ("s", 14), ("s", 15), ("w", 17), ("s", 32), ("s", 57), ("w", 0), ("y", (0, 0, 1)), ("w", 3),
    ("y", (0, 1, 0)), ("y", (1, 0, 0)), ("s", 22), ("s", 33), ("s", 19), ("s", 59), ("s", 1), ("w", 37), ("s", 50),
    ("w", 7), ("y", (0, 2, 0)), ("w", 12), ("y", (0, 3, 1)), ("y", (2, 0, 0)), ("s", 8), ("s", 64), ("s", 38),
    ("s", 28), ("w", 16), ("w", 14), ("w", 15), ("y", (0, 3, 3)), ("w", 68), ("y", (3, 3, 0)), ("s", 58), ("w", 32),
    ("s", 27), ("w", 33), ("y", (1, 3, 0)), ("s", 23), ("s", 34), ("s", 63), ("s", 18), ("w", 50), ("y", (2, 3, 0)),
    ("w", 59), ("y", (3, 1, 0)), ("s", 45), ("s", 60), ("w", 1), ("y", (0, 0, 2)), ("w", 64), ("s", 46), ("s", 55),
    ("s", 41), ("w", 8), ("y", (0, 2, 1)), ("w", 57), ("w", 58), ("y", (3, 0, 3)), ("s", 4), ("w", 38),
    ("y", (2, 0, 1)), ("w", 27), ("w", 28), ("y", (1, 2, 0)), ("s", 65), ("s", 10), ("w", 22), ("w", 23),
    ("y", (1, 1, 0)), ("w", 63), ("y", (3, 2, 0)), ("s", 51), ("w", 34), ("y", (1, 3, 1)), ("w", 18), ("w", 19),
    ("y", (1, 0, 1)), ("s", 40), ("s", 29), ("w", 45), ("w", 46), ("y", (2, 2, 0)), ("L", 0), ("s", 36), ("s", 24),
    ("s", 47), ("w", 4), ("y", (0, 1, 1)), ("w", 10), ("y", (0, 2, 3)), ("w", 29), ("y", (1, 2, 1)), ("w", 40),
    ("y", (2, 0, 3)), ("w", 41), ("y", (2, 1, 0)), ("w", 51), ("y", (2, 3, 1)), ("w", 55), ("y", (3, 0, 1)),
    ("w", 60), ("y", (3, 1, 1)), ("w", 65), ("y", (3, 2, 1)), ("s", 67), ("s", 13), ("s", 39), ("C", 0), ("s", 42),
    ("s", 62), ("s", 6), ("D", 0), ("C", 1), ("s", 69), ("w", 36), ("s", 31), ("s", 21), ("w", 24),
    ("y", (1, 1, 1)), ("y", (1, 3, 3)), ("w", 47), ("y", (2, 2, 1)), ("D", 1), ("w", 67), ("s", 49), ("w", 39),
    ("s", 52), ("s", 9), ("w", 13), ("y", (0, 3, 2)), ("y", (2, 0, 2)), ("y", (3, 2, 3)), ("C", 2), ("s", 70),
    ("s", 53), ("w", 6), ("s", 5), ("y", (0, 1, 3)), ("w", 42), ("y", (2, 1, 1)), ("w", 62), ("y", (3, 1, 3)),
    ("D", 2), ("s", 26), ("s", 71), ("w", 21), ("s", 20), ("y", (1, 0, 3)), ("w", 31), ("y", (1, 2, 3)), ("w", 69),
    ("y", (3, 3, 1)), ("C", 3), ("s", 44), ("w", 52), ("s", 48), ("s", 35), ("w", 9), ("y", (0, 2, 2)), ("w", 49),
    ("y", (2, 2, 3)), ("y", (2, 3, 2)), ("D", 3), ("s", 30), ("w", 70), ("s", 66), ("s", 61), ("w", 5),
    ("y", (0, 1, 2)), ("w", 53), ("y", (2, 3, 3)), ("y", (3, 3, 2)), ("C", 4), ("s", 56), ("s", 43), ("w", 26),
    ("s", 25), ("w", 20), ("y", (1, 0, 2)), ("y", (1, 1, 3)), ("w", 71), ("y", (3, 3, 3)), ("D", 4), ("w", 35),
    ("y", (1, 3, 2)), ("w", 44), ("y", (2, 1, 3)), ("w", 48), ("y", (2, 2, 2)), ("C", 5), ("w", 30),
    ("y", (1, 2, 2)), ("w", 61), ("y", (3, 1, 2)), ("w", 66), ("y", (3, 2, 2)), ("D", 5), ("w", 25),
    ("y", (1, 1, 2)), ("w", 43), ("y", (2, 1, 2)), ("w", 56), ("y", (3, 0, 2)),
)

PRODUCTS = [(what, int(kind == "D")) for kind, what in ACTIONS if kind in ("C", "D")]
LATE = [(group, other) for group in range(EARLY // 2, 8) for other in range(2)]


def digits(values, bits):
    return sum(value << (bits * index) for index, value in enumerate(values))


def digit(packed, index, bits):
    return lax.shift_right_logical(jnp.int32(packed), index * bits) & ((1 << bits) - 1)


def pick(products, index):
    group = digit(digits([g % 2 for g, _ in products], 1), index, 1)
    group += 2 * digit(digits([g // 2 for g, _ in products], 2), index, 2)
    return group, digit(digits([o for _, o in products], 1), index, 1)


def dims():
    chan, lag = lax.axis_index("chan"), lax.axis_index("lag")
    core, z, y_lo = chan % 2, (chan // 2) % 4, chan // 8
    x, y = lag % 4, (lag // 4) * 2 + y_lo
    return x, y, z, core


def device(x, y, z, core):
    return (((y % 2) * 4 + z) * 2 + core, (y // 2) * 4 + x)


def group_channels(coords, group, other):
    _, y, z, core = coords
    sign = (1 - 2 * core) * (1 - 2 * other)
    step = group // 2
    step = step + (step // 2) * (5 - 2 * step)
    z_there = (z + 4 + sign * (step - 4 * (step // 3))) % 4
    core_there = core + other - 2 * core * other
    return (((y + group) % 2) * 4 + z_there) * 2 + core_there


def multiply(lhs_ref, g_ref, channels):
    block = g_ref[pl.ds(channels * 8, 8)].reshape(8 * CB, CB)
    product = jnp.dot(lhs_ref[...], block, preferred_element_type=F32)
    return (product * (1.0 / math.sqrt(SAMPLES))).reshape(CB, SLOTS, CB)


def gather_kernel(
    raw_hbm, taps_hbm, map_hbm, lags_hbm, part_ref, lhs_ref, g_ref,
    raw_ref, taps_ref, map_ref, lags_ref, dec_ref, stat_ref, turned_ref, shift_ref, mixed_ref,
    raw_sem, small_sem, stat_send, stat_recv, send_sem, recv_sem, other_send, other_recv,
):
    coords = x, y, z, core = dims()
    me, lag = device(*coords)
    ahead = 1 - 2 * core

    small_copies = [
        pltpu.make_async_copy(there, here, small_sem.at[index])
        for index, (there, here) in enumerate(((taps_hbm, taps_ref), (lags_hbm, lags_ref), (map_hbm, map_ref)))
    ]
    for copy in small_copies:
        copy.start()
    raw_copies = []
    for index in range(4):
        rows = pl.ds(1280 * index, min(1280, ROWS - 1280 * index))
        raw_copies.append(pltpu.make_async_copy(raw_hbm.at[rows], raw_ref.at[rows], raw_sem.at[index]))
        raw_copies[-1].start()

    def lag_peer(step):
        return me, (lag + step) % 8

    sibling = device(x, y, z, 1 - core)
    barrier = pltpu.get_barrier_semaphore()
    peers = [lag_peer(step) for step in range(1, 8)] + [sibling]
    peers += [device(x, (y + step) % 4, z, core) for step in (1, 3)]
    peers += [device(x, y, (z + step) % 4, core) for step in (1, 3)]
    for peer in peers:
        pl.semaphore_signal(barrier, inc=1, device_id=peer, device_id_type=MESH)

    small_copies[0].wait()
    taps = jnp.broadcast_to(taps_ref[...].astype(F32), (8, TAPS)).astype(BF16)
    spread = lax.broadcasted_iota(jnp.int32, (TAPS, 256), 0) + lax.broadcasted_iota(jnp.int32, (TAPS, 256), 1)
    spread = (spread == 128 + DEC - 1).astype(F32).astype(BF16)
    first = jnp.dot(taps, spread, preferred_element_type=F32)
    first = jnp.concatenate([first, jnp.zeros((8, 512), F32)], axis=1)
    wide = lax.broadcasted_iota(jnp.int32, (8, 768), 0)
    band = first
    for step in range(1, 8):
        band = jnp.where(wide == step, pltpu.roll(first, DEC * step, 1), band)
    band = jnp.concatenate([band] + [pltpu.roll(band, 8 * DEC * step, 1) for step in range(1, 4)], axis=0)
    next_band = pltpu.roll(band[0:16, 0:256], 8, 1).astype(BF16)
    band = band.astype(BF16)

    def tail():
        last = raw_ref[4992:5000].astype(F32)
        last = jnp.concatenate([last, jnp.zeros((8, CB), F32)], axis=0).astype(BF16)
        return [last, jnp.zeros((112, CB), BF16)]

    for part in range(8):
        begin = 640 * part - 128
        if part % 2 == 0:
            raw_copies[part // 2].wait()
        if part == 0:
            piece = jnp.dot(band[:, 128:], raw_ref[0:640], preferred_element_type=F32)
        elif part == 7:
            window = jnp.concatenate([raw_ref[begin:4992]] + tail(), axis=0)
            piece = jnp.dot(band, window, preferred_element_type=F32)
        else:
            piece = jnp.dot(band, raw_ref[begin : begin + 768], preferred_element_type=F32)
        dec_ref[32 * part : 32 * part + 32] = piece
    window = jnp.concatenate([raw_ref[4864:4992]] + tail(), axis=0)
    over = jnp.dot(next_band, window, preferred_element_type=F32)[0:8]

    dec = dec_ref[...]
    sample = lax.broadcasted_iota(jnp.int32, (CB, CB), 0)
    whole = (sample >= HEAD) & (sample < STEP)
    count = STEP - HEAD
    mean = jnp.sum(jnp.where(whole, dec, 0.0), axis=0, keepdims=True) * (1.0 / count)
    spread2 = jnp.where(whole, dec - mean, 0.0)
    energy = jnp.sum(spread2 * spread2, axis=0, keepdims=True)
    line = lax.broadcasted_iota(jnp.int32, (8, CB), 0)
    stat_ref[lag] = jnp.where(
        line == 0,
        mean,
        jnp.where(
            line == 1,
            energy,
            jnp.where(line < 5, pltpu.roll(dec[0:8], 2, 0), pltpu.roll(over, 5, 0)),
        ),
    )
    pl.semaphore_wait(barrier, len(peers))

    def stat_copy(step):
        return pltpu.make_async_remote_copy(
            src_ref=stat_ref.at[lag],
            dst_ref=stat_ref.at[lag],
            send_sem=stat_send.at[step],
            recv_sem=stat_recv.at[step],
            device_id=lag_peer(step),
            device_id_type=MESH,
        )

    for step in range(1, 8):
        stat_copy(step).start()
    row = lax.broadcasted_iota(jnp.int32, (512, 256), 0)
    far = 10000
    time = jnp.where(
        row < 256,
        jnp.where(row < STEP, row, far),
        jnp.where(row < 384, jnp.where(row - 128 < STEP, row - 128 - STEP, far), row - 384 + STEP),
    )
    column = lax.broadcasted_iota(jnp.int32, (512, 256), 1)
    column = jnp.where(column < STEP, column, -far)
    time = time - column
    small_copies[1].wait()
    for slot in range(SLOTS):
        shift_ref[:, CB * slot : CB * slot + CB] = (time == -lags_ref[0:1, slot : slot + 1]).astype(F32).astype(BF16)

    order = lax.broadcasted_iota(jnp.int32, (CB, CB), 0)
    small_copies[2].wait()
    place = (map_ref[...] - (me * CB) == order).astype(F32).astype(BF16)
    for step in range(1, 8):
        stat_copy(step).wait_recv()

    stats = [stat_ref[d] for d in range(8)]
    total = jnp.zeros((8, CB), F32)
    heads = []
    before = jnp.zeros((8, CB), F32)
    for d in range(8):
        head = pltpu.roll(stats[d], 6, 0)
        if d:
            from_left = pltpu.roll(stats[d - 1], 3, 0)
            head = head + from_left
            before = before + jnp.where(lag == d, from_left, 0.0)
        heads.append(head)
        total = total + jnp.where(line < HEAD, head, 0.0)
    mean = count * sum(s[0:1] for s in stats) + jnp.sum(total, axis=0, keepdims=True)
    mean = mean * (1.0 / SAMPLES)
    energy = jnp.zeros((1, CB), F32)
    total = jnp.zeros((8, CB), F32)
    for d in range(8):
        away = stats[d][0:1] - mean
        energy = energy + stats[d][1:2] + count * (away * away)
        away = jnp.where(line < HEAD, heads[d] - mean, 0.0)
        total = total + away * away
    energy = (energy + jnp.sum(total, axis=0, keepdims=True)) * (1.0 / SAMPLES)
    scale = lax.rsqrt(energy + 1e-05)
    dec_ref[0:8] = dec_ref[0:8] + jnp.where(line < HEAD, before, 0.0)
    white = jnp.where(sample < STEP, (dec_ref[...] - mean) * scale, 0.0).astype(BF16)
    ordered = lax.dot_general(white, place, (((1,), (1,)), ((), ())), preferred_element_type=F32)

    there = (0, 1, 2, -1)
    at_x = [(x + 4 + ahead * k) % 4 for k in there]
    at_y = [(y + 4 + ahead * k) % 4 for k in there]
    at_z = [(z + 4 + ahead * k) % 4 for k in there]
    term_y = [(k % 2) * 64 + (k // 2) * 4 for k in at_y]
    term_z = [k * 16 + core * 8 for k in at_z]

    def place_of(offset):
        return at_x[offset[0]] + term_y[offset[1]] + term_z[offset[2]]

    neighbours = {}
    for step in (1, 3):
        neighbours[0, step] = device(at_x[step], y, z, core)
        neighbours[1, step] = device(x, at_y[step], z, core)
        neighbours[2, step] = device(x, y, at_z[step], core)

    g_ref[place_of((0, 0, 0))] = ordered.astype(BF16)

    def block_copy(index):
        offset, axis, row, rows = COPIES[index]
        sent = list(offset)
        sent[axis] = {1: 0, 3: 0, 2: 3}[offset[axis]]
        to = 3 if offset[axis] == 1 else 1
        here = g_ref.at[place_of(sent), pl.ds(row, rows)]
        return pltpu.make_async_remote_copy(
            src_ref=here, dst_ref=here, send_sem=send_sem, recv_sem=recv_sem.at[index],
            device_id=neighbours[axis, to], device_id_type=MESH,
        )

    def block_wait(index):
        offset, axis, row, rows = COPIES[index]
        here = g_ref.at[place_of(offset), pl.ds(row, rows)]
        pltpu.make_async_copy(here, here, recv_sem.at[index]).wait()

    def hand_over(offset):
        here = g_ref.at[place_of(offset)]
        group = (at_y[offset[1]] % 2) * 4 + at_z[offset[2]]
        pltpu.make_async_remote_copy(
            src_ref=here, dst_ref=here, send_sem=other_send, recv_sem=other_recv.at[group],
            device_id=sibling, device_id_type=MESH,
        ).start()

    def taken_over(group):
        channels = group_channels(coords, group, True)
        here = g_ref.at[pl.ds(channels * 8, 8)]
        pltpu.make_async_copy(here, here, other_recv.at[channels // 2]).wait()

    def build_own():
        eye = lax.broadcasted_iota(jnp.int32, (CB, CB), 0) == lax.broadcasted_iota(jnp.int32, (CB, CB), 1)
        eye = eye.astype(F32).astype(BF16)
        turned_ref[0] = jnp.zeros((CB, CB), BF16)
        turned_ref[9] = jnp.zeros((CB, CB), BF16)

        def turn(d, carry):
            turned = lax.dot_general(eye, g_ref[me * 8 + d], (((1,), (1,)), ((), ())), preferred_element_type=F32)
            turned_ref[d + 1] = turned.astype(BF16)
            return carry

        lax.fori_loop(0, 8, turn, 0)

        def shift(d, carry):
            around = jnp.concatenate(
                [turned_ref[d + 1], turned_ref[d, :, 128:256], turned_ref[d + 2, :, 0:128]], axis=1
            )
            moved = jnp.dot(around, shift_ref[...], preferred_element_type=F32)
            for slot in range(SLOTS):
                for half in range(2):
                    begin = CB * slot + 128 * half
                    mixed_ref[half, pl.ds(slot, CB, stride=SLOTS), :] = moved[:, begin : begin + 128]
            for half in range(2):
                there = pl.ds(pl.multiple_of(d * CB + 128 * half, 128), 128)
                lhs_ref[:, there] = mixed_ref[half].astype(BF16)
            return carry

        lax.fori_loop(0, 8, shift, 0)

    def act(actions):
        for kind, what in actions:
            if kind == "w":
                block_wait(what)
            elif kind == "s":
                block_copy(what).start()
            elif kind == "y":
                hand_over(what)
            elif kind == "L":
                build_own()
            elif kind == "D":
                taken_over(what)

    spans, span = [], []
    for action in ACTIONS:
        span.append(action)
        if action[0] in ("C", "D"):
            spans.append(span)
            span = []

    act(spans[0])

    def product(index, carry):
        for number in range(1, len(spans)):
            pl.when(index == number)(functools.partial(act, spans[number]))
        group, other = pick(PRODUCTS, index)
        part_ref[2 * group + other] = multiply(lhs_ref, g_ref, group_channels(coords, group, other))
        return carry

    lax.fori_loop(0, EARLY, product, 0)
    act(span)
    for group in range(EARLY // 2, 8):
        taken_over(group)

    for step in range(1, 8):
        stat_copy(step).wait_send()
    gone = g_ref.at[pl.ds(0, 63)]
    pltpu.make_async_copy(gone, gone, send_sem).wait()
    gone = g_ref.at[pl.ds(0, 64)]
    pltpu.make_async_copy(gone, gone, other_send).wait()


def finish_kernel(part_ref, lhs_ref, g_ref, out_ref, stage_ref, part_sem, stage_sem):
    coords = dims()

    def columns(group, other):
        channels = group_channels(coords, group, other)
        return out_ref.at[:, :, pl.ds(pl.multiple_of(channels * CB, CB), CB)]

    def early_copy(index):
        return pltpu.make_async_copy(part_ref.at[index], columns(index // 2, index % 2), part_sem.at[index])

    def late_copy(index):
        return pltpu.make_async_copy(stage_ref.at[index], columns(*pick(LATE, index)), stage_sem.at[index])

    def early(index, carry):
        early_copy(index).start()
        return carry

    def late(index, carry):
        stage_ref[index] = multiply(lhs_ref, g_ref, group_channels(coords, *pick(LATE, index)))
        late_copy(index).start()
        return carry

    def early_end(index, carry):
        early_copy(index).wait()
        return carry

    def late_end(index, carry):
        late_copy(index).wait()
        return carry

    lax.fori_loop(0, EARLY, early, 0)
    lax.fori_loop(0, len(LATE), late, 0)
    lax.fori_loop(0, EARLY, early_end, 0)
    lax.fori_loop(0, len(LATE), late_end, 0)


def local(raw, fir_taps, channel_map, lag_offsets):
    vmem = pl.BlockSpec(memory_space=pltpu.VMEM)
    given = (raw.T, fir_taps.reshape(1, TAPS), channel_map.reshape(1, CB), lag_offsets.reshape(1, SLOTS))
    hbm = pl.BlockSpec(memory_space=pltpu.HBM)
    part, lhs, blocks = pl.pallas_call(
        gather_kernel,
        out_shape=[
            pltpu.VMEM((EARLY, CB, SLOTS, CB), F32),
            pltpu.VMEM((CB * SLOTS, 8 * CB), BF16),
            pltpu.VMEM((128, CB, CB), BF16),
        ],
        in_specs=[hbm] * 4,
        out_specs=[vmem] * 3,
        scratch_shapes=[
            pltpu.VMEM((ROWS, CB), BF16),
            pltpu.VMEM((1, TAPS), BF16),
            pltpu.VMEM((1, CB), jnp.int32),
            pltpu.VMEM((1, SLOTS), jnp.int32),
            pltpu.VMEM((CB, CB), F32),
            pltpu.VMEM((8, 8, CB), F32),
            pltpu.VMEM((10, CB, CB), BF16),
            pltpu.VMEM((512, SLOTS * CB), BF16),
            pltpu.VMEM((2, CB * SLOTS, 128), F32),
            pltpu.SemaphoreType.DMA((4,)),
            pltpu.SemaphoreType.DMA((3,)),
            pltpu.SemaphoreType.DMA((8,)),
            pltpu.SemaphoreType.DMA((8,)),
            pltpu.SemaphoreType.DMA,
            pltpu.SemaphoreType.DMA((len(COPIES),)),
            pltpu.SemaphoreType.DMA,
            pltpu.SemaphoreType.DMA((8,)),
        ],
        compiler_params=pltpu.CompilerParams(collective_id=0, has_side_effects=True, vmem_limit_bytes=14 << 20),
        name="gather",
    )(*[pltpu.with_memory_space_constraint(a, pltpu.HBM) for a in given])
    part, lhs, blocks = [pltpu.with_memory_space_constraint(a, pltpu.VMEM) for a in (part, lhs, blocks)]
    return pl.pallas_call(
        finish_kernel,
        out_shape=jax.ShapeDtypeStruct((CB, SLOTS, CHANNELS), F32),
        in_specs=[vmem] * 3,
        out_specs=pl.BlockSpec(memory_space=pltpu.HBM),
        scratch_shapes=[
            pltpu.VMEM((len(LATE), CB, SLOTS, CB), F32),
            pltpu.SemaphoreType.DMA((EARLY,)),
            pltpu.SemaphoreType.DMA((len(LATE),)),
        ],
        compiler_params=pltpu.CompilerParams(vmem_limit_bytes=(len(LATE) + 3) << 20),
        name="finish",
    )(part, lhs, blocks)


def solution(mesh):
    placed = (P("chan", "lag"), P(), P("chan"), P("lag"))
    return jax.shard_map(
        local, mesh=mesh, in_specs=placed, out_specs=P("chan", "lag", None), check_vma=False
    )
```

time: 82.9 us -> 68.4 us (0.83)
  the two profiles are of different devices: /device:TPU:0 before, /device:TPU:1 now
where the time goes in v2:
time: 68.4 us; the launch traced here: 68.3 us
  Pallas kernels  68.3 us (100%)
    pallas_call x1, Pallas kernels, local(): pl.pallas_call(gather_kernel, out_shape=[pltpu.VMEM((EARLY, CB, SLOTS, CB...  61.5 us
    pallas_call x1, Pallas kernels, local(): pl.pallas_call(finish_kernel, out_shape=jax.ShapeDtypeStruct((CB, SLOTS,...  6.8 us

profile of v2, /device:TPU:1, one launch (start us, length us, event | category | flops | bytes accessed | tf_op | source)
XLA Modules:
  0.0 68.3 jit_solution(17778163283610451223)
XLA Ops:
  0.0 61.5 %gather.1 = (f32[12,256,4,256]{3,2,1,0:T(4,128)S(1)}, bf16[1024,2048]{1,0:T(8,128)(2,1)S(1)}, bf16[128,256,256]{2,1,0:T(8,128)(2,1)S(1)}) custom-call(bf16[5000,256]{1,0:T(8,128)(2,1)} %bitcast.4, bf16[1,80]{1,0:T(2,128)(2,1)} %bitcast.6, s32[1,256]{1,0:T(1,128)} %bitcast.5, s32[1,4]{1,0:T(1,128)} %bitcast.7), custom_call_target="tpu_custom_call" | custom-call | tf_op jit(solution)/shard_map/gather/pallas_call | solution.py:422
  61.5 6.8 %finish.1 = f32[256,4,4096]{2,1,0:T(4,128)} custom-call(f32[12,256,4,256]{3,2,1,0:T(4,128)S(1)} %get-tuple-element.8.part_ref, bf16[1024,2048]{1,0:T(8,128)(2,1)S(1)} %get-tuple-element.9.lhs_ref, bf16[128,256,256]{2,1,0:T(8,128)(2,1)S(1)} %get-tuple-element.10.g_ref), custom_call_target="tpu_custom_call" | custom-call | tf_op jit(solution)/shard_map/finish/pallas_call | solution.py:454

commit v3 on v2

--- a/solution.py
+++ b/solution.py
@@ -21,59 +21,69 @@
 ROWS = 5000
 F32, BF16 = jnp.float32, jnp.bfloat16
 
-EARLY = 12
 COPIES = (
-    ((0, 0, 1), 2, 0, 256), ((0, 0, 2), 2, 0, 256), ((0, 0, 3), 2, 0, 256), ((0, 1, 0), 1, 0, 256),
-    ((0, 1, 1), 2, 0, 256), ((0, 1, 2), 2, 0, 256), ((0, 1, 3), 2, 0, 256), ((0, 2, 0), 1, 0, 256),
-    ((0, 2, 1), 1, 0, 256), ((0, 2, 2), 2, 0, 256), ((0, 2, 3), 1, 0, 256), ((0, 3, 0), 1, 0, 256),
-    ((0, 3, 1), 2, 0, 256), ((0, 3, 2), 1, 0, 256), ((0, 3, 3), 2, 0, 80), ((0, 3, 3), 2, 160, 96),
-    ((0, 3, 3), 1, 80, 80), ((1, 0, 0), 0, 0, 256), ((1, 0, 1), 0, 0, 160), ((1, 0, 1), 2, 160, 96),
-    ((1, 0, 2), 2, 0, 256), ((1, 0, 3), 2, 0, 256), ((1, 1, 0), 1, 0, 80), ((1, 1, 0), 0, 80, 176),
-    ((1, 1, 1), 1, 0, 256), ((1, 1, 2), 2, 0, 256), ((1, 1, 3), 0, 0, 256), ((1, 2, 0), 1, 0, 160),
-    ((1, 2, 0), 0, 160, 96), ((1, 2, 1), 1, 0, 256), ((1, 2, 2), 0, 0, 256), ((1, 2, 3), 1, 0, 256),
-    ((1, 3, 0), 1, 0, 160), ((1, 3, 0), 0, 160, 96), ((1, 3, 1), 2, 0, 256), ((1, 3, 2), 2, 0, 256),
-    ((1, 3, 3), 0, 0, 256), ((2, 0, 0), 0, 0, 256), ((2, 0, 1), 2, 0, 256), ((2, 0, 2), 2, 0, 256),
-    ((2, 0, 3), 0, 0, 256), ((2, 1, 0), 1, 0, 256), ((2, 1, 1), 0, 0, 256), ((2, 1, 2), 1, 0, 256),
-    ((2, 1, 3), 0, 0, 256), ((2, 2, 0), 1, 0, 160), ((2, 2, 0), 0, 160, 96), ((2, 2, 1), 2, 0, 256),
-    ((2, 2, 2), 1, 0, 256), ((2, 2, 3), 0, 0, 256), ((2, 3, 0), 1, 0, 256), ((2, 3, 1), 2, 0, 256),
-    ((2, 3, 2), 1, 0, 256), ((2, 3, 3), 1, 0, 256), ((3, 0, 0), 0, 0, 256), ((3, 0, 1), 0, 0, 256),
-    ((3, 0, 2), 0, 0, 256), ((3, 0, 3), 2, 0, 160), ((3, 0, 3), 0, 160, 96), ((3, 1, 0), 0, 0, 256),
-    ((3, 1, 1), 2, 0, 256), ((3, 1, 2), 2, 0, 256), ((3, 1, 3), 1, 0, 256), ((3, 2, 0), 1, 0, 160),
-    ((3, 2, 0), 0, 160, 96), ((3, 2, 1), 0, 0, 256), ((3, 2, 2), 1, 0, 256), ((3, 2, 3), 0, 0, 256),
-    ((3, 3, 0), 0, 0, 256), ((3, 3, 1), 0, 0, 256), ((3, 3, 2), 0, 0, 256), ((3, 3, 3), 1, 0, 256),
+    ((0, 0, 1), 2, 0, 80), ((0, 0, 1), 2, 80, 80), ((0, 0, 1), 2, 160, 96), ((0, 0, 2), 2, 0, 256),
+    ((0, 0, 3), 2, 0, 80), ((0, 0, 3), 2, 80, 80), ((0, 0, 3), 2, 160, 96), ((0, 1, 0), 1, 0, 80),
+    ((0, 1, 0), 1, 80, 80), ((0, 1, 0), 1, 160, 96), ((0, 1, 1), 1, 0, 80), ((0, 1, 1), 2, 80, 176),
+    ((0, 1, 2), 1, 0, 256), ((0, 1, 3), 2, 0, 256), ((0, 2, 0), 1, 0, 256), ((0, 2, 1), 2, 0, 256),
+    ((0, 2, 2), 1, 0, 256), ((0, 2, 3), 2, 0, 256), ((0, 3, 0), 1, 0, 80), ((0, 3, 0), 1, 80, 80),
+    ((0, 3, 0), 1, 160, 96), ((0, 3, 1), 2, 0, 256), ((0, 3, 2), 2, 0, 256), ((0, 3, 3), 2, 0, 256),
+    ((1, 0, 0), 0, 0, 80), ((1, 0, 0), 0, 80, 80), ((1, 0, 0), 0, 160, 96), ((1, 0, 1), 2, 0, 256),
+    ((1, 0, 2), 0, 0, 256), ((1, 0, 3), 0, 0, 160), ((1, 0, 3), 2, 160, 96), ((1, 1, 0), 1, 0, 256),
+    ((1, 1, 1), 1, 0, 256), ((1, 1, 2), 0, 0, 256), ((1, 1, 3), 0, 0, 256), ((1, 2, 0), 1, 0, 256),
+    ((1, 2, 1), 1, 0, 256), ((1, 2, 2), 2, 0, 80), ((1, 2, 2), 1, 80, 176), ((1, 2, 3), 2, 0, 256),
+    ((1, 3, 0), 1, 0, 256), ((1, 3, 1), 2, 0, 256), ((1, 3, 2), 1, 0, 256), ((1, 3, 3), 1, 0, 256),
+    ((2, 0, 0), 0, 0, 256), ((2, 0, 1), 2, 0, 256), ((2, 0, 2), 2, 0, 256), ((2, 0, 3), 0, 0, 256),
+    ((2, 1, 0), 1, 0, 160), ((2, 1, 0), 0, 160, 96), ((2, 1, 1), 0, 0, 256), ((2, 1, 2), 0, 0, 256),
+    ((2, 1, 3), 2, 0, 256), ((2, 2, 0), 1, 0, 160), ((2, 2, 0), 0, 160, 96), ((2, 2, 1), 2, 0, 256),
+    ((2, 2, 2), 2, 0, 256), ((2, 2, 3), 1, 0, 256), ((2, 3, 0), 0, 0, 80), ((2, 3, 0), 0, 160, 96),
+    ((2, 3, 0), 1, 80, 80), ((2, 3, 1), 2, 0, 256), ((2, 3, 2), 2, 0, 256), ((2, 3, 3), 1, 0, 256),
+    ((3, 0, 0), 0, 0, 80), ((3, 0, 0), 0, 80, 80), ((3, 0, 0), 0, 160, 96), ((3, 0, 1), 0, 0, 80),
+    ((3, 0, 1), 0, 160, 96), ((3, 0, 1), 2, 80, 80), ((3, 0, 2), 0, 0, 256), ((3, 0, 3), 0, 0, 80),
+    ((3, 0, 3), 0, 160, 96), ((3, 0, 3), 2, 80, 80), ((3, 1, 0), 0, 0, 256), ((3, 1, 1), 2, 0, 256),
+    ((3, 1, 2), 0, 0, 256), ((3, 1, 3), 0, 0, 256), ((3, 2, 0), 0, 0, 80), ((3, 2, 0), 0, 160, 96),
+    ((3, 2, 0), 1, 80, 80), ((3, 2, 1), 1, 0, 80), ((3, 2, 1), 0, 80, 176), ((3, 2, 2), 2, 0, 256),
+    ((3, 2, 3), 2, 0, 256), ((3, 3, 0), 0, 0, 80), ((3, 3, 0), 0, 160, 96), ((3, 3, 0), 1, 80, 80),
+    ((3, 3, 1), 1, 0, 80), ((3, 3, 1), 2, 80, 176), ((3, 3, 2), 1, 0, 256), ((3, 3, 3), 1, 0, 80),
+    ((3, 3, 3), 2, 80, 80), ((3, 3, 3), 0, 160, 96),
 )
 ACTIONS = (
-    ("s", 54), ("s", 11), ("s", 2), ("y", (0, 0, 0)), ("s", 17), ("s", 3), ("s", 0), ("w", 54), ("s", 37),
-    ("w", 11), ("s", 7), ("s", 12), ("w", 2), ("y", (0, 0, 3)), ("y", (0, 3, 0)), ("y", (3, 0, 0)), ("s", 68),
-    ("s", 16), ("s", 14), ("s", 15), ("w", 17), ("s", 32), ("s", 57), ("w", 0), ("y", (0, 0, 1)), ("w", 3),
-    ("y", (0, 1, 0)), ("y", (1, 0, 0)), ("s", 22), ("s", 33), ("s", 19), ("s", 59), ("s", 1), ("w", 37), ("s", 50),
-    ("w", 7), ("y", (0, 2, 0)), ("w", 12), ("y", (0, 3, 1)), ("y", (2, 0, 0)), ("s", 8), ("s", 64), ("s", 38),
-    ("s", 28), ("w", 16), ("w", 14), ("w", 15), ("y", (0, 3, 3)), ("w", 68), ("y", (3, 3, 0)), ("s", 58), ("w", 32),
-    ("s", 27), ("w", 33), ("y", (1, 3, 0)), ("s", 23), ("s", 34), ("s", 63), ("s", 18), ("w", 50), ("y", (2, 3, 0)),
-    ("w", 59), ("y", (3, 1, 0)), ("s", 45), ("s", 60), ("w", 1), ("y", (0, 0, 2)), ("w", 64), ("s", 46), ("s", 55),
-    ("s", 41), ("w", 8), ("y", (0, 2, 1)), ("w", 57), ("w", 58), ("y", (3, 0, 3)), ("s", 4), ("w", 38),
-    ("y", (2, 0, 1)), ("w", 27), ("w", 28), ("y", (1, 2, 0)), ("s", 65), ("s", 10), ("w", 22), ("w", 23),
-    ("y", (1, 1, 0)), ("w", 63), ("y", (3, 2, 0)), ("s", 51), ("w", 34), ("y", (1, 3, 1)), ("w", 18), ("w", 19),
-    ("y", (1, 0, 1)), ("s", 40), ("s", 29), ("w", 45), ("w", 46), ("y", (2, 2, 0)), ("L", 0), ("s", 36), ("s", 24),
-    ("s", 47), ("w", 4), ("y", (0, 1, 1)), ("w", 10), ("y", (0, 2, 3)), ("w", 29), ("y", (1, 2, 1)), ("w", 40),
-    ("y", (2, 0, 3)), ("w", 41), ("y", (2, 1, 0)), ("w", 51), ("y", (2, 3, 1)), ("w", 55), ("y", (3, 0, 1)),
-    ("w", 60), ("y", (3, 1, 1)), ("w", 65), ("y", (3, 2, 1)), ("s", 67), ("s", 13), ("s", 39), ("C", 0), ("s", 42),
-    ("s", 62), ("s", 6), ("D", 0), ("C", 1), ("s", 69), ("w", 36), ("s", 31), ("s", 21), ("w", 24),
-    ("y", (1, 1, 1)), ("y", (1, 3, 3)), ("w", 47), ("y", (2, 2, 1)), ("D", 1), ("w", 67), ("s", 49), ("w", 39),
-    ("s", 52), ("s", 9), ("w", 13), ("y", (0, 3, 2)), ("y", (2, 0, 2)), ("y", (3, 2, 3)), ("C", 2), ("s", 70),
-    ("s", 53), ("w", 6), ("s", 5), ("y", (0, 1, 3)), ("w", 42), ("y", (2, 1, 1)), ("w", 62), ("y", (3, 1, 3)),
-    ("D", 2), ("s", 26), ("s", 71), ("w", 21), ("s", 20), ("y", (1, 0, 3)), ("w", 31), ("y", (1, 2, 3)), ("w", 69),
-    ("y", (3, 3, 1)), ("C", 3), ("s", 44), ("w", 52), ("s", 48), ("s", 35), ("w", 9), ("y", (0, 2, 2)), ("w", 49),
-    ("y", (2, 2, 3)), ("y", (2, 3, 2)), ("D", 3), ("s", 30), ("w", 70), ("s", 66), ("s", 61), ("w", 5),
-    ("y", (0, 1, 2)), ("w", 53), ("y", (2, 3, 3)), ("y", (3, 3, 2)), ("C", 4), ("s", 56), ("s", 43), ("w", 26),
-    ("s", 25), ("w", 20), ("y", (1, 0, 2)), ("y", (1, 1, 3)), ("w", 71), ("y", (3, 3, 3)), ("D", 4), ("w", 35),
-    ("y", (1, 3, 2)), ("w", 44), ("y", (2, 1, 3)), ("w", 48), ("y", (2, 2, 2)), ("C", 5), ("w", 30),
-    ("y", (1, 2, 2)), ("w", 61), ("y", (3, 1, 2)), ("w", 66), ("y", (3, 2, 2)), ("D", 5), ("w", 25),
-    ("y", (1, 1, 2)), ("w", 43), ("y", (2, 1, 2)), ("w", 56), ("y", (3, 0, 2)),
+    ("s", 64), ("s", 18), ("s", 0), ("s", 65), ("s", 19), ("s", 4), ("s", 66), ("s", 20), ("s", 6), ("s", 24),
+    ("s", 7), ("s", 2), ("s", 25), ("s", 8), ("s", 1), ("s", 26), ("s", 9), ("s", 5), ("y", (0, 0, 0)), ("w", 18),
+    ("s", 85), ("w", 0), ("s", 10), ("s", 67), ("w", 65), ("s", 87), ("s", 73), ("w", 4), ("s", 71), ("s", 69),
+    ("w", 64), ("w", 66), ("s", 44), ("w", 19), ("w", 20), ("s", 14), ("s", 21), ("s", 86), ("s", 23), ("w", 6),
+    ("s", 72), ("y", (0, 3, 0)), ("y", (3, 0, 0)), ("w", 2), ("s", 68), ("w", 1), ("y", (0, 0, 1)), ("w", 24),
+    ("w", 25), ("w", 26), ("s", 40), ("s", 27), ("w", 8), ("w", 9), ("w", 7), ("s", 74), ("s", 31), ("s", 11),
+    ("w", 5), ("s", 29), ("s", 3), ("s", 30), ("s", 13), ("y", (0, 0, 3)), ("y", (0, 1, 0)), ("y", (1, 0, 0)),
+    ("w", 85), ("s", 58), ("w", 67), ("s", 88), ("w", 87), ("s", 92), ("s", 80), ("w", 71), ("s", 91), ("w", 14),
+    ("s", 79), ("s", 15), ("s", 78), ("w", 44), ("s", 60), ("s", 45), ("s", 48), ("s", 17), ("y", (0, 2, 0)),
+    ("w", 21), ("y", (0, 3, 1)), ("y", (2, 0, 0)), ("w", 86), ("y", (3, 3, 0)), ("s", 59), ("s", 89), ("w", 72),
+    ("w", 73), ("s", 47), ("w", 40), ("s", 35), ("s", 41), ("y", (1, 3, 0)), ("y", (3, 0, 3)), ("w", 23), ("s", 93),
+    ("s", 22), ("y", (0, 3, 3)), ("w", 68), ("w", 69), ("y", (3, 0, 1)), ("w", 31), ("y", (1, 1, 0)), ("w", 27),
+    ("s", 32), ("y", (1, 0, 1)), ("w", 74), ("s", 49), ("w", 88), ("s", 81), ("s", 75), ("y", (3, 1, 0)), ("w", 10),
+    ("w", 11), ("y", (0, 1, 1)), ("w", 58), ("w", 60), ("s", 53), ("w", 79), ("s", 54), ("w", 3), ("s", 28),
+    ("s", 12), ("w", 80), ("w", 78), ("s", 84), ("s", 70), ("y", (0, 0, 2)), ("y", (3, 2, 0)), ("w", 29), ("w", 30),
+    ("s", 43), ("w", 59), ("s", 61), ("y", (1, 0, 3)), ("y", (2, 3, 0)), ("w", 35), ("s", 39), ("y", (1, 2, 0)),
+    ("w", 13), ("s", 34), ("w", 47), ("s", 63), ("s", 46), ("s", 77), ("y", (0, 1, 3)), ("y", (2, 0, 3)), ("w", 91),
+    ("w", 92), ("w", 93), ("y", (3, 3, 3)), ("w", 32), ("y", (1, 1, 1)), ("w", 48), ("w", 49), ("s", 52),
+    ("y", (2, 1, 0)), ("w", 15), ("s", 82), ("y", (0, 2, 1)), ("w", 53), ("w", 54), ("s", 55), ("y", (2, 2, 0)),
+    ("L", 0), ("w", 12), ("s", 76), ("w", 41), ("s", 36), ("w", 63), ("s", 62), ("s", 33), ("s", 57), ("w", 28),
+    ("s", 42), ("w", 70), ("s", 90), ("y", (0, 1, 2)), ("w", 17), ("y", (0, 2, 3)), ("y", (1, 0, 2)), ("w", 34),
+    ("y", (1, 1, 3)), ("y", (1, 3, 1)), ("w", 43), ("y", (1, 3, 3)), ("w", 45), ("y", (2, 0, 1)), ("y", (2, 3, 3)),
+    ("y", (3, 0, 2)), ("w", 77), ("y", (3, 1, 3)), ("w", 81), ("w", 82), ("y", (3, 2, 1)), ("w", 89),
+    ("y", (3, 3, 1)), ("w", 22), ("s", 16), ("y", (0, 3, 2)), ("C", 1), ("w", 75), ("s", 50), ("y", (3, 1, 1)),
+    ("C", 0), ("w", 84), ("s", 83), ("y", (3, 2, 3)), ("D", 1), ("w", 76), ("s", 51), ("w", 36), ("y", (1, 2, 1)),
+    ("w", 61), ("y", (2, 3, 1)), ("y", (3, 1, 2)), ("w", 39), ("s", 37), ("w", 57), ("s", 56), ("w", 33),
+    ("y", (1, 1, 2)), ("y", (1, 2, 3)), ("y", (2, 2, 3)), ("D", 0), ("w", 42), ("s", 38), ("y", (1, 3, 2)),
+    ("w", 46), ("y", (2, 0, 2)), ("w", 50), ("y", (2, 1, 1)), ("C", 4), ("w", 52), ("y", (2, 1, 3)), ("w", 90),
+    ("y", (3, 3, 2)), ("D", 4), ("w", 16), ("y", (0, 2, 2)), ("w", 51), ("y", (2, 1, 2)), ("w", 55),
+    ("y", (2, 2, 1)), ("C", 3), ("w", 62), ("y", (2, 3, 2)), ("D", 3), ("w", 37), ("w", 38), ("y", (1, 2, 2)),
+    ("w", 83), ("y", (3, 2, 2)), ("C", 5), ("w", 56), ("y", (2, 2, 2)), ("D", 5), ("C", 2),
 )
 
 PRODUCTS = [(what, int(kind == "D")) for kind, what in ACTIONS if kind in ("C", "D")]
-LATE = [(group, other) for group in range(EARLY // 2, 8) for other in range(2)]
+LATE = [(group, other) for group in range(8) for other in range(2) if (group, other) not in PRODUCTS]
+EARLY = len(PRODUCTS)
 
 
 def digits(values, bits):
@@ -145,7 +155,7 @@
     barrier = pltpu.get_barrier_semaphore()
     peers = [lag_peer(step) for step in range(1, 8)] + [sibling]
     peers += [device(x, (y + step) % 4, z, core) for step in (1, 3)]
-    peers += [device(x, y, (z + step) % 4, core) for step in (1, 3)]
+    peers += [device(x, y, (z + step) % 4, core) for step in (1, 2, 3)]
     for peer in peers:
         pl.semaphore_signal(barrier, inc=1, device_id=peer, device_id_type=MESH)
 
@@ -272,18 +282,21 @@
         return at_x[offset[0]] + term_y[offset[1]] + term_z[offset[2]]
 
     neighbours = {}
-    for step in (1, 3):
+    for step in (1, 2, 3):
         neighbours[0, step] = device(at_x[step], y, z, core)
         neighbours[1, step] = device(x, at_y[step], z, core)
         neighbours[2, step] = device(x, y, at_z[step], core)
 
     g_ref[place_of((0, 0, 0))] = ordered.astype(BF16)
+    turned_ref[0] = jnp.zeros((CB, CB), BF16)
+    turned_ref[9] = jnp.zeros((CB, CB), BF16)
 
     def block_copy(index):
         offset, axis, row, rows = COPIES[index]
+        axis, far = axis % 3, axis // 3
         sent = list(offset)
-        sent[axis] = {1: 0, 3: 0, 2: 3}[offset[axis]]
-        to = 3 if offset[axis] == 1 else 1
+        sent[axis] = {1: 0, 3: 0, 2: 0 if far else 3}[offset[axis]]
+        to = 2 if far else 3 if offset[axis] == 1 else 1
         here = g_ref.at[place_of(sent), pl.ds(row, rows)]
         return pltpu.make_async_remote_copy(
             src_ref=here, dst_ref=here, send_sem=send_sem, recv_sem=recv_sem.at[index],
@@ -308,34 +321,32 @@
         here = g_ref.at[pl.ds(channels * 8, 8)]
         pltpu.make_async_copy(here, here, other_recv.at[channels // 2]).wait()
 
+    eye = lax.broadcasted_iota(jnp.int32, (CB, CB), 0) == lax.broadcasted_iota(jnp.int32, (CB, CB), 1)
+    eye = eye.astype(F32).astype(BF16)
+
+    def turn(offset):
+        block = g_ref[place_of(offset)]
+        turned = lax.dot_general(eye, block, (((1,), (1,)), ((), ())), preferred_element_type=F32)
+        turned_ref[(at_y[offset[1]] // 2) * 4 + at_x[offset[0]] + 1] = turned.astype(BF16)
+
     def build_own():
-        eye = lax.broadcasted_iota(jnp.int32, (CB, CB), 0) == lax.broadcasted_iota(jnp.int32, (CB, CB), 1)
-        eye = eye.astype(F32).astype(BF16)
-        turned_ref[0] = jnp.zeros((CB, CB), BF16)
-        turned_ref[9] = jnp.zeros((CB, CB), BF16)
-
-        def turn(d, carry):
-            turned = lax.dot_general(eye, g_ref[me * 8 + d], (((1,), (1,)), ((), ())), preferred_element_type=F32)
-            turned_ref[d + 1] = turned.astype(BF16)
+        def shift(pair, carry):
+            for part in range(2):
+                d = pair * 2 + part
+                around = jnp.concatenate(
+                    [turned_ref[d + 1], turned_ref[d, :, 128:256], turned_ref[d + 2, :, 0:128]], axis=1
+                )
+                moved = jnp.dot(around, shift_ref[...], preferred_element_type=F32)
+                for slot in range(SLOTS):
+                    for half in range(2):
+                        begin = CB * slot + 128 * half
+                        mixed_ref[2 * part + half, pl.ds(slot, CB, stride=SLOTS), :] = moved[:, begin : begin + 128]
+                for half in range(2):
+                    there = pl.ds(pl.multiple_of(d * CB + 128 * half, 128), 128)
+                    lhs_ref[:, there] = mixed_ref[2 * part + half].astype(BF16)
             return carry
 
-        lax.fori_loop(0, 8, turn, 0)
-
-        def shift(d, carry):
-            around = jnp.concatenate(
-                [turned_ref[d + 1], turned_ref[d, :, 128:256], turned_ref[d + 2, :, 0:128]], axis=1
-            )
-            moved = jnp.dot(around, shift_ref[...], preferred_element_type=F32)
-            for slot in range(SLOTS):
-                for half in range(2):
-                    begin = CB * slot + 128 * half
-                    mixed_ref[half, pl.ds(slot, CB, stride=SLOTS), :] = moved[:, begin : begin + 128]
-            for half in range(2):
-                there = pl.ds(pl.multiple_of(d * CB + 128 * half, 128), 128)
-                lhs_ref[:, there] = mixed_ref[half].astype(BF16)
-            return carry
-
-        lax.fori_loop(0, 8, shift, 0)
+        lax.fori_loop(0, 4, shift, 0)
 
     def act(actions):
         for kind, what in actions:
@@ -345,6 +356,8 @@
                 block_copy(what).start()
             elif kind == "y":
                 hand_over(what)
+                if what[1] in (0, 2) and what[2] == 0:
+                    turn(what)
             elif kind == "L":
                 build_own()
             elif kind == "D":
@@ -363,13 +376,14 @@
         for number in range(1, len(spans)):
             pl.when(index == number)(functools.partial(act, spans[number]))
         group, other = pick(PRODUCTS, index)
-        part_ref[2 * group + other] = multiply(lhs_ref, g_ref, group_channels(coords, group, other))
+        part_ref[index] = multiply(lhs_ref, g_ref, group_channels(coords, group, other))
         return carry
 
     lax.fori_loop(0, EARLY, product, 0)
     act(span)
-    for group in range(EARLY // 2, 8):
-        taken_over(group)
+    for group, other in LATE:
+        if other:
+            taken_over(group)
 
     for step in range(1, 8):
         stat_copy(step).wait_send()
@@ -387,7 +401,7 @@
         return out_ref.at[:, :, pl.ds(pl.multiple_of(channels * CB, CB), CB)]
 
     def early_copy(index):
-        return pltpu.make_async_copy(part_ref.at[index], columns(index // 2, index % 2), part_sem.at[index])
+        return pltpu.make_async_copy(part_ref.at[index], columns(*pick(PRODUCTS, index)), part_sem.at[index])
 
     def late_copy(index):
         return pltpu.make_async_copy(stage_ref.at[index], columns(*pick(LATE, index)), stage_sem.at[index])
@@ -437,7 +451,7 @@
             pltpu.VMEM((8, 8, CB), F32),
             pltpu.VMEM((10, CB, CB), BF16),
             pltpu.VMEM((512, SLOTS * CB), BF16),
-            pltpu.VMEM((2, CB * SLOTS, 128), F32),
+            pltpu.VMEM((4, CB * SLOTS, 128), F32),
             pltpu.SemaphoreType.DMA((4,)),
             pltpu.SemaphoreType.DMA((3,)),
             pltpu.SemaphoreType.DMA((8,)),

time: 68.4 us -> 64.1 us (0.937)
  the two profiles are of different devices: /device:TPU:1 before, /device:TPU:0 now
where the time goes in v3:
time: 64.1 us; the launch traced here: 63.9 us
  Pallas kernels  63.9 us (100%)
    pallas_call x1, Pallas kernels, local(): pl.pallas_call(gather_kernel, out_shape=[pltpu.VMEM((EARLY, CB, SLOTS, CB...  55.9 us
    pallas_call x1, Pallas kernels, local(): pl.pallas_call(finish_kernel, out_shape=jax.ShapeDtypeStruct((CB, SLOTS,...  7.99 us

profile of v3, /device:TPU:0, one launch (start us, length us, event | category | flops | bytes accessed | tf_op | source)
XLA Modules:
  0.0 63.9 jit_solution(9167629570205420617)
XLA Ops:
  0.0 55.9 %gather.1 = (f32[11,256,4,256]{3,2,1,0:T(4,128)S(1)}, bf16[1024,2048]{1,0:T(8,128)(2,1)S(1)}, bf16[128,256,256]{2,1,0:T(8,128)(2,1)S(1)}) custom-call(bf16[5000,256]{1,0:T(8,128)(2,1)} %bitcast.4, bf16[1,80]{1,0:T(2,128)(2,1)} %bitcast.6, s32[1,256]{1,0:T(1,128)} %bitcast.5, s32[1,4]{1,0:T(1,128)} %bitcast.7), custom_call_target="tpu_custom_call" | custom-call | tf_op jit(solution)/shard_map/gather/pallas_call | solution.py:436
  56.0 8.0 %finish.1 = f32[256,4,4096]{2,1,0:T(4,128)} custom-call(f32[11,256,4,256]{3,2,1,0:T(4,128)S(1)} %get-tuple-element.8.part_ref, bf16[1024,2048]{1,0:T(8,128)(2,1)S(1)} %get-tuple-element.9.lhs_ref, bf16[128,256,256]{2,1,0:T(8,128)(2,1)S(1)} %get-tuple-element.10.g_ref), custom_call_target="tpu_custom_call" | custom-call | tf_op jit(solution)/shard_map/finish/pallas_call | solution.py:468

commit v4 on v3

--- a/solution.py
+++ b/solution.py
@@ -24,61 +24,51 @@
 COPIES = (
     ((0, 0, 1), 2, 0, 80), ((0, 0, 1), 2, 80, 80), ((0, 0, 1), 2, 160, 96), ((0, 0, 2), 2, 0, 256),
     ((0, 0, 3), 2, 0, 80), ((0, 0, 3), 2, 80, 80), ((0, 0, 3), 2, 160, 96), ((0, 1, 0), 1, 0, 80),
-    ((0, 1, 0), 1, 80, 80), ((0, 1, 0), 1, 160, 96), ((0, 1, 1), 1, 0, 80), ((0, 1, 1), 2, 80, 176),
-    ((0, 1, 2), 1, 0, 256), ((0, 1, 3), 2, 0, 256), ((0, 2, 0), 1, 0, 256), ((0, 2, 1), 2, 0, 256),
-    ((0, 2, 2), 1, 0, 256), ((0, 2, 3), 2, 0, 256), ((0, 3, 0), 1, 0, 80), ((0, 3, 0), 1, 80, 80),
-    ((0, 3, 0), 1, 160, 96), ((0, 3, 1), 2, 0, 256), ((0, 3, 2), 2, 0, 256), ((0, 3, 3), 2, 0, 256),
+    ((0, 1, 0), 1, 80, 80), ((0, 1, 0), 1, 160, 96), ((0, 1, 1), 2, 0, 256), ((0, 1, 2), 2, 0, 256),
+    ((0, 1, 3), 2, 0, 256), ((0, 2, 0), 1, 0, 256), ((0, 2, 1), 1, 0, 256), ((0, 2, 2), 1, 0, 256),
+    ((0, 2, 3), 2, 0, 256), ((0, 3, 0), 1, 0, 80), ((0, 3, 0), 1, 80, 80), ((0, 3, 0), 1, 160, 96),
+    ((0, 3, 1), 1, 0, 80), ((0, 3, 1), 2, 80, 176), ((0, 3, 2), 1, 0, 256), ((0, 3, 3), 2, 0, 256),
     ((1, 0, 0), 0, 0, 80), ((1, 0, 0), 0, 80, 80), ((1, 0, 0), 0, 160, 96), ((1, 0, 1), 2, 0, 256),
-    ((1, 0, 2), 0, 0, 256), ((1, 0, 3), 0, 0, 160), ((1, 0, 3), 2, 160, 96), ((1, 1, 0), 1, 0, 256),
-    ((1, 1, 1), 1, 0, 256), ((1, 1, 2), 0, 0, 256), ((1, 1, 3), 0, 0, 256), ((1, 2, 0), 1, 0, 256),
-    ((1, 2, 1), 1, 0, 256), ((1, 2, 2), 2, 0, 80), ((1, 2, 2), 1, 80, 176), ((1, 2, 3), 2, 0, 256),
-    ((1, 3, 0), 1, 0, 256), ((1, 3, 1), 2, 0, 256), ((1, 3, 2), 1, 0, 256), ((1, 3, 3), 1, 0, 256),
-    ((2, 0, 0), 0, 0, 256), ((2, 0, 1), 2, 0, 256), ((2, 0, 2), 2, 0, 256), ((2, 0, 3), 0, 0, 256),
-    ((2, 1, 0), 1, 0, 160), ((2, 1, 0), 0, 160, 96), ((2, 1, 1), 0, 0, 256), ((2, 1, 2), 0, 0, 256),
-    ((2, 1, 3), 2, 0, 256), ((2, 2, 0), 1, 0, 160), ((2, 2, 0), 0, 160, 96), ((2, 2, 1), 2, 0, 256),
-    ((2, 2, 2), 2, 0, 256), ((2, 2, 3), 1, 0, 256), ((2, 3, 0), 0, 0, 80), ((2, 3, 0), 0, 160, 96),
-    ((2, 3, 0), 1, 80, 80), ((2, 3, 1), 2, 0, 256), ((2, 3, 2), 2, 0, 256), ((2, 3, 3), 1, 0, 256),
-    ((3, 0, 0), 0, 0, 80), ((3, 0, 0), 0, 80, 80), ((3, 0, 0), 0, 160, 96), ((3, 0, 1), 0, 0, 80),
-    ((3, 0, 1), 0, 160, 96), ((3, 0, 1), 2, 80, 80), ((3, 0, 2), 0, 0, 256), ((3, 0, 3), 0, 0, 80),
-    ((3, 0, 3), 0, 160, 96), ((3, 0, 3), 2, 80, 80), ((3, 1, 0), 0, 0, 256), ((3, 1, 1), 2, 0, 256),
-    ((3, 1, 2), 0, 0, 256), ((3, 1, 3), 0, 0, 256), ((3, 2, 0), 0, 0, 80), ((3, 2, 0), 0, 160, 96),
-    ((3, 2, 0), 1, 80, 80), ((3, 2, 1), 1, 0, 80), ((3, 2, 1), 0, 80, 176), ((3, 2, 2), 2, 0, 256),
-    ((3, 2, 3), 2, 0, 256), ((3, 3, 0), 0, 0, 80), ((3, 3, 0), 0, 160, 96), ((3, 3, 0), 1, 80, 80),
-    ((3, 3, 1), 1, 0, 80), ((3, 3, 1), 2, 80, 176), ((3, 3, 2), 1, 0, 256), ((3, 3, 3), 1, 0, 80),
-    ((3, 3, 3), 2, 80, 80), ((3, 3, 3), 0, 160, 96),
+    ((1, 0, 2), 2, 0, 256), ((1, 0, 3), 0, 0, 80), ((1, 0, 3), 2, 80, 176), ((1, 1, 0), 1, 0, 160),
+    ((1, 1, 0), 0, 160, 96), ((1, 1, 1), 0, 0, 256), ((1, 1, 2), 0, 0, 256), ((1, 1, 3), 1, 0, 256),
+    ((1, 2, 0), 1, 0, 80), ((1, 2, 0), 0, 80, 176), ((1, 2, 1), 0, 0, 256), ((1, 2, 2), 0, 0, 256),
+    ((1, 2, 3), 1, 0, 256), ((1, 3, 0), 1, 0, 256), ((1, 3, 1), 1, 0, 80), ((1, 3, 1), 1, 160, 96),
+    ((1, 3, 1), 2, 80, 80), ((1, 3, 2), 1, 0, 256), ((1, 3, 3), 1, 0, 256), ((2, 0, 0), 0, 0, 256),
+    ((2, 0, 1), 2, 0, 80), ((2, 0, 1), 0, 80, 176), ((2, 0, 2), 2, 0, 256), ((2, 0, 3), 0, 0, 256),
+    ((2, 1, 0), 0, 0, 256), ((2, 1, 1), 2, 0, 256), ((2, 1, 2), 2, 0, 256), ((2, 1, 3), 2, 0, 256),
+    ((2, 2, 0), 1, 0, 80), ((2, 2, 0), 0, 80, 176), ((2, 2, 1), 1, 0, 256), ((2, 2, 2), 2, 0, 256),
+    ((2, 2, 3), 1, 0, 256), ((2, 3, 0), 0, 0, 80), ((2, 3, 0), 1, 80, 176), ((2, 3, 1), 1, 0, 256),
+    ((2, 3, 2), 2, 0, 256), ((2, 3, 3), 1, 0, 256), ((3, 0, 0), 0, 0, 80), ((3, 0, 0), 0, 80, 80),
+    ((3, 0, 0), 0, 160, 96), ((3, 0, 1), 2, 0, 160), ((3, 0, 1), 0, 160, 96), ((3, 0, 2), 2, 0, 256),
+    ((3, 0, 3), 0, 0, 160), ((3, 0, 3), 2, 160, 96), ((3, 1, 0), 1, 0, 256), ((3, 1, 1), 0, 0, 256),
+    ((3, 1, 2), 1, 0, 256), ((3, 1, 3), 0, 0, 256), ((3, 2, 0), 1, 0, 160), ((3, 2, 0), 0, 160, 96),
+    ((3, 2, 1), 0, 0, 256), ((3, 2, 2), 0, 0, 256), ((3, 2, 3), 2, 0, 256), ((3, 3, 0), 0, 0, 80),
+    ((3, 3, 0), 0, 160, 96), ((3, 3, 0), 1, 80, 80), ((3, 3, 1), 2, 0, 256), ((3, 3, 2), 0, 0, 256),
+    ((3, 3, 3), 2, 0, 256),
 )
 ACTIONS = (
-    ("s", 64), ("s", 18), ("s", 0), ("s", 65), ("s", 19), ("s", 4), ("s", 66), ("s", 20), ("s", 6), ("s", 24),
-    ("s", 7), ("s", 2), ("s", 25), ("s", 8), ("s", 1), ("s", 26), ("s", 9), ("s", 5), ("y", (0, 0, 0)), ("w", 18),
-    ("s", 85), ("w", 0), ("s", 10), ("s", 67), ("w", 65), ("s", 87), ("s", 73), ("w", 4), ("s", 71), ("s", 69),
-    ("w", 64), ("w", 66), ("s", 44), ("w", 19), ("w", 20), ("s", 14), ("s", 21), ("s", 86), ("s", 23), ("w", 6),
-    ("s", 72), ("y", (0, 3, 0)), ("y", (3, 0, 0)), ("w", 2), ("s", 68), ("w", 1), ("y", (0, 0, 1)), ("w", 24),
-    ("w", 25), ("w", 26), ("s", 40), ("s", 27), ("w", 8), ("w", 9), ("w", 7), ("s", 74), ("s", 31), ("s", 11),
-    ("w", 5), ("s", 29), ("s", 3), ("s", 30), ("s", 13), ("y", (0, 0, 3)), ("y", (0, 1, 0)), ("y", (1, 0, 0)),
-    ("w", 85), ("s", 58), ("w", 67), ("s", 88), ("w", 87), ("s", 92), ("s", 80), ("w", 71), ("s", 91), ("w", 14),
-    ("s", 79), ("s", 15), ("s", 78), ("w", 44), ("s", 60), ("s", 45), ("s", 48), ("s", 17), ("y", (0, 2, 0)),
-    ("w", 21), ("y", (0, 3, 1)), ("y", (2, 0, 0)), ("w", 86), ("y", (3, 3, 0)), ("s", 59), ("s", 89), ("w", 72),
-    ("w", 73), ("s", 47), ("w", 40), ("s", 35), ("s", 41), ("y", (1, 3, 0)), ("y", (3, 0, 3)), ("w", 23), ("s", 93),
-    ("s", 22), ("y", (0, 3, 3)), ("w", 68), ("w", 69), ("y", (3, 0, 1)), ("w", 31), ("y", (1, 1, 0)), ("w", 27),
-    ("s", 32), ("y", (1, 0, 1)), ("w", 74), ("s", 49), ("w", 88), ("s", 81), ("s", 75), ("y", (3, 1, 0)), ("w", 10),
-    ("w", 11), ("y", (0, 1, 1)), ("w", 58), ("w", 60), ("s", 53), ("w", 79), ("s", 54), ("w", 3), ("s", 28),
-    ("s", 12), ("w", 80), ("w", 78), ("s", 84), ("s", 70), ("y", (0, 0, 2)), ("y", (3, 2, 0)), ("w", 29), ("w", 30),
-    ("s", 43), ("w", 59), ("s", 61), ("y", (1, 0, 3)), ("y", (2, 3, 0)), ("w", 35), ("s", 39), ("y", (1, 2, 0)),
-    ("w", 13), ("s", 34), ("w", 47), ("s", 63), ("s", 46), ("s", 77), ("y", (0, 1, 3)), ("y", (2, 0, 3)), ("w", 91),
-    ("w", 92), ("w", 93), ("y", (3, 3, 3)), ("w", 32), ("y", (1, 1, 1)), ("w", 48), ("w", 49), ("s", 52),
-    ("y", (2, 1, 0)), ("w", 15), ("s", 82), ("y", (0, 2, 1)), ("w", 53), ("w", 54), ("s", 55), ("y", (2, 2, 0)),
-    ("L", 0), ("w", 12), ("s", 76), ("w", 41), ("s", 36), ("w", 63), ("s", 62), ("s", 33), ("s", 57), ("w", 28),
-    ("s", 42), ("w", 70), ("s", 90), ("y", (0, 1, 2)), ("w", 17), ("y", (0, 2, 3)), ("y", (1, 0, 2)), ("w", 34),
-    ("y", (1, 1, 3)), ("y", (1, 3, 1)), ("w", 43), ("y", (1, 3, 3)), ("w", 45), ("y", (2, 0, 1)), ("y", (2, 3, 3)),
-    ("y", (3, 0, 2)), ("w", 77), ("y", (3, 1, 3)), ("w", 81), ("w", 82), ("y", (3, 2, 1)), ("w", 89),
-    ("y", (3, 3, 1)), ("w", 22), ("s", 16), ("y", (0, 3, 2)), ("C", 1), ("w", 75), ("s", 50), ("y", (3, 1, 1)),
-    ("C", 0), ("w", 84), ("s", 83), ("y", (3, 2, 3)), ("D", 1), ("w", 76), ("s", 51), ("w", 36), ("y", (1, 2, 1)),
-    ("w", 61), ("y", (2, 3, 1)), ("y", (3, 1, 2)), ("w", 39), ("s", 37), ("w", 57), ("s", 56), ("w", 33),
-    ("y", (1, 1, 2)), ("y", (1, 2, 3)), ("y", (2, 2, 3)), ("D", 0), ("w", 42), ("s", 38), ("y", (1, 3, 2)),
-    ("w", 46), ("y", (2, 0, 2)), ("w", 50), ("y", (2, 1, 1)), ("C", 4), ("w", 52), ("y", (2, 1, 3)), ("w", 90),
-    ("y", (3, 3, 2)), ("D", 4), ("w", 16), ("y", (0, 2, 2)), ("w", 51), ("y", (2, 1, 2)), ("w", 55),
-    ("y", (2, 2, 1)), ("C", 3), ("w", 62), ("y", (2, 3, 2)), ("D", 3), ("w", 37), ("w", 38), ("y", (1, 2, 2)),
-    ("w", 83), ("y", (3, 2, 2)), ("C", 5), ("w", 56), ("y", (2, 2, 2)), ("D", 5), ("C", 2),
+    ("s", 67), ("s", 17), ("s", 2), ("s", 66), ("s", 18), ("s", 0), ("s", 68), ("s", 19), ("s", 4), ("s", 24),
+    ("s", 9), ("s", 5), ("s", 25), ("s", 7), ("s", 6), ("s", 26), ("s", 8), ("s", 1), ("w", 67), ("s", 85),
+    ("w", 17), ("s", 83), ("w", 2), ("s", 70), ("w", 66), ("s", 69), ("w", 0), ("s", 20), ("w", 68), ("s", 47),
+    ("w", 18), ("w", 19), ("s", 13), ("s", 21), ("s", 84), ("s", 74), ("s", 73), ("w", 4), ("s", 29), ("s", 23),
+    ("w", 5), ("s", 72), ("w", 9), ("s", 32), ("w", 24), ("w", 25), ("s", 31), ("w", 6), ("s", 3), ("w", 26),
+    ("s", 41), ("s", 30), ("w", 8), ("w", 7), ("s", 10), ("s", 27), ("s", 12), ("w", 83), ("s", 61), ("w", 85),
+    ("s", 78), ("w", 69), ("w", 70), ("s", 49), ("w", 20), ("w", 21), ("s", 14), ("w", 47), ("s", 62), ("s", 48),
+    ("w", 13), ("s", 79), ("s", 16), ("s", 37), ("y", (0, 0)), ("w", 74), ("s", 52), ("w", 84), ("s", 86),
+    ("w", 72), ("w", 73), ("s", 51), ("s", 88), ("s", 71), ("w", 61), ("s", 56), ("w", 3), ("s", 22), ("w", 41),
+    ("s", 36), ("s", 44), ("w", 29), ("w", 30), ("s", 46), ("s", 28), ("s", 35), ("w", 78), ("w", 79), ("s", 57),
+    ("s", 82), ("w", 10), ("s", 33), ("s", 75), ("w", 14), ("s", 38), ("s", 80), ("w", 27), ("s", 42), ("s", 43),
+    ("w", 62), ("y", (3, 0)), ("w", 52), ("s", 53), ("s", 55), ("w", 31), ("w", 32), ("y", (1, 0)), ("w", 12),
+    ("s", 77), ("s", 11), ("w", 51), ("s", 65), ("s", 50), ("y", (0, 3)), ("w", 48), ("w", 49), ("s", 63),
+    ("w", 22), ("s", 87), ("s", 15), ("w", 1), ("y", (0, 1)), ("w", 36), ("w", 37), ("w", 56), ("w", 57),
+    ("y", (2, 0)), ("L", 0), ("w", 46), ("s", 40), ("C", 1), ("w", 65), ("s", 60), ("s", 64), ("w", 71), ("s", 76),
+    ("w", 23), ("w", 88), ("y", (3, 3)), ("D", 1), ("w", 63), ("s", 58), ("w", 28), ("s", 45), ("w", 42), ("w", 43),
+    ("w", 44), ("w", 86), ("y", (3, 1)), ("w", 15), ("s", 39), ("s", 81), ("C", 0), ("D", 0), ("w", 60), ("s", 59),
+    ("w", 33), ("w", 53), ("w", 75), ("y", (1, 1)), ("w", 16), ("w", 40), ("w", 82), ("y", (2, 3)), ("w", 35),
+    ("w", 55), ("w", 77), ("y", (1, 3)), ("s", 54), ("C", 3), ("w", 11), ("s", 34), ("C", 4), ("w", 38), ("w", 58),
+    ("w", 80), ("y", (2, 1)), ("w", 50), ("y", (0, 2)), ("C", 5), ("w", 45), ("w", 64), ("w", 87), ("y", (3, 2)),
+    ("D", 3), ("w", 39), ("w", 59), ("w", 81), ("y", (2, 2)), ("D", 4), ("w", 34), ("w", 54), ("w", 76),
+    ("y", (1, 2)), ("D", 5), ("C", 2),
 )
 
 PRODUCTS = [(what, int(kind == "D")) for kind, what in ACTIONS if kind in ("C", "D")]
@@ -308,45 +298,61 @@
         here = g_ref.at[place_of(offset), pl.ds(row, rows)]
         pltpu.make_async_copy(here, here, recv_sem.at[index]).wait()
 
+    def line_of(offset):
+        return pl.ds(term_y[offset[0]] + term_z[offset[1]], 4)
+
     def hand_over(offset):
-        here = g_ref.at[place_of(offset)]
-        group = (at_y[offset[1]] % 2) * 4 + at_z[offset[2]]
+        here = g_ref.at[line_of(offset)]
+        half = (at_y[offset[0]] % 2) * 4 + at_z[offset[1]] + 8 * (at_y[offset[0]] // 2)
         pltpu.make_async_remote_copy(
-            src_ref=here, dst_ref=here, send_sem=other_send, recv_sem=other_recv.at[group],
+            src_ref=here, dst_ref=here, send_sem=other_send, recv_sem=other_recv.at[half],
             device_id=sibling, device_id_type=MESH,
         ).start()
 
     def taken_over(group):
         channels = group_channels(coords, group, True)
-        here = g_ref.at[pl.ds(channels * 8, 8)]
-        pltpu.make_async_copy(here, here, other_recv.at[channels // 2]).wait()
+        for half in range(2):
+            here = g_ref.at[pl.ds(channels * 8 + 4 * half, 4)]
+            pltpu.make_async_copy(here, here, other_recv.at[channels // 2 + 8 * half]).wait()
 
     eye = lax.broadcasted_iota(jnp.int32, (CB, CB), 0) == lax.broadcasted_iota(jnp.int32, (CB, CB), 1)
     eye = eye.astype(F32).astype(BF16)
 
     def turn(offset):
-        block = g_ref[place_of(offset)]
-        turned = lax.dot_general(eye, block, (((1,), (1,)), ((), ())), preferred_element_type=F32)
-        turned_ref[(at_y[offset[1]] // 2) * 4 + at_x[offset[0]] + 1] = turned.astype(BF16)
-
-    def build_own():
-        def shift(pair, carry):
-            for part in range(2):
-                d = pair * 2 + part
-                around = jnp.concatenate(
-                    [turned_ref[d + 1], turned_ref[d, :, 128:256], turned_ref[d + 2, :, 0:128]], axis=1
-                )
-                moved = jnp.dot(around, shift_ref[...], preferred_element_type=F32)
-                for slot in range(SLOTS):
-                    for half in range(2):
-                        begin = CB * slot + 128 * half
-                        mixed_ref[2 * part + half, pl.ds(slot, CB, stride=SLOTS), :] = moved[:, begin : begin + 128]
+        first = (at_y[offset[0]] // 2) * 4
+        for part in range(4):
+            block = g_ref[me * 8 + first + part]
+            turned = lax.dot_general(eye, block, (((1,), (1,)), ((), ())), preferred_element_type=F32)
+            turned_ref[first + part + 1] = turned.astype(BF16)
+
+    def shift(*pair):
+        for part, d in enumerate(pair):
+            around = jnp.concatenate(
+                [turned_ref[d + 1], turned_ref[d, :, 128:256], turned_ref[d + 2, :, 0:128]], axis=1
+            )
+            moved = jnp.dot(around, shift_ref[...], preferred_element_type=F32)
+            for slot in range(SLOTS):
                 for half in range(2):
-                    there = pl.ds(pl.multiple_of(d * CB + 128 * half, 128), 128)
-                    lhs_ref[:, there] = mixed_ref[2 * part + half].astype(BF16)
+                    begin = CB * slot + 128 * half
+                    mixed_ref[2 * part + half, pl.ds(slot, CB, stride=SLOTS), :] = moved[:, begin : begin + 128]
+            for half in range(2):
+                there = pl.ds(pl.multiple_of(d * CB + 128 * half, 128), 128)
+                lhs_ref[:, there] = mixed_ref[2 * part + half].astype(BF16)
+
+    def shift_first():
+        inner = (y // 2) * 4 + 1
+        shift(inner, inner + 1)
+
+    def shift_rest():
+        inner = (1 - y // 2) * 4 + 1
+
+        def step(index, carry):
+            first = jnp.where(index == 0, inner, jnp.where(index == 1, 3, 0))
+            second = jnp.where(index == 0, inner + 1, jnp.where(index == 1, 4, 7))
+            shift(first, second)
             return carry
 
-        lax.fori_loop(0, 4, shift, 0)
+        lax.fori_loop(0, 3, step, 0)
 
     def act(actions):
         for kind, what in actions:
@@ -356,10 +362,12 @@
                 block_copy(what).start()
             elif kind == "y":
                 hand_over(what)
-                if what[1] in (0, 2) and what[2] == 0:
+                if what in ((0, 0), (2, 0)):
                     turn(what)
+                if what == (0, 0):
+                    shift_first()
             elif kind == "L":
-                build_own()
+                shift_rest()
             elif kind == "D":
                 taken_over(what)
 
@@ -459,7 +467,7 @@
             pltpu.SemaphoreType.DMA,
             pltpu.SemaphoreType.DMA((len(COPIES),)),
             pltpu.SemaphoreType.DMA,
-            pltpu.SemaphoreType.DMA((8,)),
+            pltpu.SemaphoreType.DMA((16,)),
         ],
         compiler_params=pltpu.CompilerParams(collective_id=0, has_side_effects=True, vmem_limit_bytes=14 << 20),
         name="gather",

time: 64.1 us -> 63.5 us (level)
  no operation moved by 1% of the time
where the time goes in v4:
time: 63.5 us; the launch traced here: 63.4 us
  Pallas kernels  63.4 us (100%)
    pallas_call x1, Pallas kernels, local(): pl.pallas_call(gather_kernel, out_shape=[pltpu.VMEM((EARLY, CB, SLOTS, CB...  55.4 us
    pallas_call x1, Pallas kernels, local(): pl.pallas_call(finish_kernel, out_shape=jax.ShapeDtypeStruct((CB, SLOTS,...  7.98 us

profile of v4, /device:TPU:0, one launch (start us, length us, event | category | flops | bytes accessed | tf_op | source)
XLA Modules:
  0.0 63.4 jit_solution(18093918818662500596)
XLA Ops:
  0.0 55.4 %gather.1 = (f32[11,256,4,256]{3,2,1,0:T(4,128)S(1)}, bf16[1024,2048]{1,0:T(8,128)(2,1)S(1)}, bf16[128,256,256]{2,1,0:T(8,128)(2,1)S(1)}) custom-call(bf16[5000,256]{1,0:T(8,128)(2,1)} %bitcast.4, bf16[1,80]{1,0:T(2,128)(2,1)} %bitcast.6, s32[1,256]{1,0:T(1,128)} %bitcast.5, s32[1,4]{1,0:T(1,128)} %bitcast.7), custom_call_target="tpu_custom_call" | custom-call | tf_op jit(solution)/shard_map/gather/pallas_call | solution.py:444
  55.4 8.0 %finish.1 = f32[256,4,4096]{2,1,0:T(4,128)} custom-call(f32[11,256,4,256]{3,2,1,0:T(4,128)S(1)} %get-tuple-element.8.part_ref, bf16[1024,2048]{1,0:T(8,128)(2,1)S(1)} %get-tuple-element.9.lhs_ref, bf16[128,256,256]{2,1,0:T(8,128)(2,1)S(1)} %get-tuple-element.10.g_ref), custom_call_target="tpu_custom_call" | custom-call | tf_op jit(solution)/shard_map/finish/pallas_call | solution.py:476

commit v5 on v4

--- a/solution.py
+++ b/solution.py
@@ -55,20 +55,20 @@
     ("s", 41), ("s", 30), ("w", 8), ("w", 7), ("s", 10), ("s", 27), ("s", 12), ("w", 83), ("s", 61), ("w", 85),
     ("s", 78), ("w", 69), ("w", 70), ("s", 49), ("w", 20), ("w", 21), ("s", 14), ("w", 47), ("s", 62), ("s", 48),
     ("w", 13), ("s", 79), ("s", 16), ("s", 37), ("y", (0, 0)), ("w", 74), ("s", 52), ("w", 84), ("s", 86),
-    ("w", 72), ("w", 73), ("s", 51), ("s", 88), ("s", 71), ("w", 61), ("s", 56), ("w", 3), ("s", 22), ("w", 41),
-    ("s", 36), ("s", 44), ("w", 29), ("w", 30), ("s", 46), ("s", 28), ("s", 35), ("w", 78), ("w", 79), ("s", 57),
-    ("s", 82), ("w", 10), ("s", 33), ("s", 75), ("w", 14), ("s", 38), ("s", 80), ("w", 27), ("s", 42), ("s", 43),
-    ("w", 62), ("y", (3, 0)), ("w", 52), ("s", 53), ("s", 55), ("w", 31), ("w", 32), ("y", (1, 0)), ("w", 12),
-    ("s", 77), ("s", 11), ("w", 51), ("s", 65), ("s", 50), ("y", (0, 3)), ("w", 48), ("w", 49), ("s", 63),
-    ("w", 22), ("s", 87), ("s", 15), ("w", 1), ("y", (0, 1)), ("w", 36), ("w", 37), ("w", 56), ("w", 57),
-    ("y", (2, 0)), ("L", 0), ("w", 46), ("s", 40), ("C", 1), ("w", 65), ("s", 60), ("s", 64), ("w", 71), ("s", 76),
-    ("w", 23), ("w", 88), ("y", (3, 3)), ("D", 1), ("w", 63), ("s", 58), ("w", 28), ("s", 45), ("w", 42), ("w", 43),
-    ("w", 44), ("w", 86), ("y", (3, 1)), ("w", 15), ("s", 39), ("s", 81), ("C", 0), ("D", 0), ("w", 60), ("s", 59),
-    ("w", 33), ("w", 53), ("w", 75), ("y", (1, 1)), ("w", 16), ("w", 40), ("w", 82), ("y", (2, 3)), ("w", 35),
-    ("w", 55), ("w", 77), ("y", (1, 3)), ("s", 54), ("C", 3), ("w", 11), ("s", 34), ("C", 4), ("w", 38), ("w", 58),
-    ("w", 80), ("y", (2, 1)), ("w", 50), ("y", (0, 2)), ("C", 5), ("w", 45), ("w", 64), ("w", 87), ("y", (3, 2)),
-    ("D", 3), ("w", 39), ("w", 59), ("w", 81), ("y", (2, 2)), ("D", 4), ("w", 34), ("w", 54), ("w", 76),
-    ("y", (1, 2)), ("D", 5), ("C", 2),
+    ("w", 72), ("w", 73), ("s", 51), ("s", 88), ("w", 61), ("s", 56), ("w", 3), ("s", 22), ("s", 71), ("w", 41),
+    ("s", 36), ("w", 29), ("w", 30), ("s", 46), ("s", 35), ("w", 78), ("w", 79), ("s", 57), ("s", 44), ("s", 82),
+    ("w", 10), ("s", 33), ("s", 75), ("w", 14), ("s", 38), ("s", 80), ("s", 28), ("w", 27), ("s", 42), ("s", 43),
+    ("w", 62), ("y", (3, 0)), ("w", 31), ("w", 32), ("w", 52), ("y", (1, 0)), ("s", 53), ("w", 12), ("s", 77),
+    ("w", 51), ("s", 65), ("y", (0, 3)), ("w", 48), ("w", 49), ("s", 63), ("w", 22), ("s", 87), ("s", 15),
+    ("s", 55), ("w", 1), ("y", (0, 1)), ("w", 36), ("w", 37), ("w", 56), ("w", 57), ("y", (2, 0)), ("L", 0),
+    ("w", 46), ("s", 40), ("s", 11), ("s", 50), ("C", 1), ("w", 65), ("s", 60), ("s", 64), ("w", 71), ("s", 76),
+    ("w", 23), ("w", 88), ("y", (3, 3)), ("D", 1), ("w", 63), ("s", 58), ("w", 42), ("w", 43), ("w", 44), ("w", 86),
+    ("y", (3, 1)), ("w", 15), ("s", 39), ("s", 81), ("C", 0), ("w", 28), ("s", 45), ("D", 0), ("w", 60), ("s", 59),
+    ("w", 55), ("s", 54), ("w", 33), ("w", 53), ("w", 75), ("y", (1, 1)), ("w", 16), ("w", 40), ("w", 82),
+    ("y", (2, 3)), ("w", 35), ("w", 77), ("y", (1, 3)), ("C", 3), ("w", 11), ("s", 34), ("C", 4), ("w", 38),
+    ("w", 58), ("w", 80), ("y", (2, 1)), ("w", 50), ("y", (0, 2)), ("C", 5), ("w", 45), ("w", 64), ("w", 87),
+    ("y", (3, 2)), ("D", 3), ("w", 39), ("w", 59), ("w", 81), ("y", (2, 2)), ("D", 4), ("w", 34), ("w", 54),
+    ("w", 76), ("y", (1, 2)), ("D", 5), ("C", 2),
 )
 
 PRODUCTS = [(what, int(kind == "D")) for kind, what in ACTIONS if kind in ("C", "D")]

time: 63.5 us -> 63.5 us (level)
  no operation moved by 1% of the time
where the time goes in v5:
time: 63.5 us; the launch traced here: 63.4 us
  Pallas kernels  63.3 us (100%)
    pallas_call x1, Pallas kernels, local(): pl.pallas_call(gather_kernel, out_shape=[pltpu.VMEM((EARLY, CB, SLOTS, CB...  55.4 us
    pallas_call x1, Pallas kernels, local(): pl.pallas_call(finish_kernel, out_shape=jax.ShapeDtypeStruct((CB, SLOTS,...  7.99 us

profile of v5, /device:TPU:0, one launch (start us, length us, event | category | flops | bytes accessed | tf_op | source)
XLA Modules:
  0.0 63.4 jit_solution(6890373435212749111)
XLA Ops:
  0.0 55.4 %gather.1 = (f32[11,256,4,256]{3,2,1,0:T(4,128)S(1)}, bf16[1024,2048]{1,0:T(8,128)(2,1)S(1)}, bf16[128,256,256]{2,1,0:T(8,128)(2,1)S(1)}) custom-call(bf16[5000,256]{1,0:T(8,128)(2,1)} %bitcast.4, bf16[1,80]{1,0:T(2,128)(2,1)} %bitcast.6, s32[1,256]{1,0:T(1,128)} %bitcast.5, s32[1,4]{1,0:T(1,128)} %bitcast.7), custom_call_target="tpu_custom_call" | custom-call | tf_op jit(solution)/shard_map/gather/pallas_call | solution.py:444
  55.4 8.0 %finish.1 = f32[256,4,4096]{2,1,0:T(4,128)} custom-call(f32[11,256,4,256]{3,2,1,0:T(4,128)S(1)} %get-tuple-element.8.part_ref, bf16[1024,2048]{1,0:T(8,128)(2,1)S(1)} %get-tuple-element.9.lhs_ref, bf16[128,256,256]{2,1,0:T(8,128)(2,1)S(1)} %get-tuple-element.10.g_ref), custom_call_target="tpu_custom_call" | custom-call | tf_op jit(solution)/shard_map/finish/pallas_call | solution.py:476
